TPU v7x, 256 devices: a whole 4x4x8 slice. The times are simulated.
256 devices in a mesh: rows: 2 (over core), trans: 16 (over x, z_hi), gvec: 8 (over y, z_lo).
Axes of the slice: x: 4, y: 4, z: 8 (z_hi: 4, z_lo: 2; z = z_hi * 2 + z_lo), core: 2. Of those that a mesh axis runs over, the one named last changes fastest.
Arguments:
- pair_density: bfloat16 [2, 16384, 4096], P(None, 'trans', 'gvec'), may hold values from -0.75 to 0.75
- coulomb: float32 [4096], P('gvec'), may hold values from 0.1 to 10
- block_index: int32 [2], P('rows'), parts along dimension 0, may hold values from 0 to 15
Outputs:
- kernel_rows: bfloat16 [2, 2048, 16384], P(None, ('rows', 'gvec'), 'trans'), parts along dimension 1
- mirrored: bfloat16 [2, 16384, 2048], P(None, 'trans', 'rows'), parts along dimension 2
There are 2 independent parts, one for each index of `rows`. A program takes and returns all parts, laid end to end along the dimension named above; an argument that names none is the same for every part. Nothing has to cross between parts.
All inputs are finite; a program needn't handle non-finite values.
Results may differ from a plain program's by a relative error of at most 0.017.
Values may be sent and summed in bfloat16 or wider, within the bound.
No kernel may reach another device: no remote copies, remote signals or barrier semaphores. Data moves between devices by JAX's collectives and lax.ppermute only.
A program may use at most 64 MiB of HBM per device.

v0:
```python
import jax
import jax.numpy as jnp
from jax import lax
from jax.sharding import PartitionSpec as P


def from_root(value, axis, source):
    kept = jnp.where(lax.axis_index(axis) == source, value, 0).astype(value.dtype)
    return lax.psum(kept, axis)


def contract(left, right):
    return lax.dot_general(
        left, right, (((1,), (1,)), ((), ())), preferred_element_type=jnp.float32
    )


def body(pair_density, coulomb, block_index):
    block = from_root(pair_density, "trans", block_index[0])
    weighted = (block.astype(jnp.float32) * coulomb[None, None, :]).astype(jnp.bfloat16)
    real_part = contract(weighted[0], pair_density[0]) + contract(weighted[1], pair_density[1])
    imag_part = contract(weighted[0], pair_density[1]) - contract(weighted[1], pair_density[0])
    partial_terms = jnp.stack([real_part, imag_part])
    kernel_rows = lax.psum_scatter(
        partial_terms.astype(jnp.bfloat16), "gvec", scatter_dimension=1, tiled=True
    )
    gathered = lax.all_gather(kernel_rows, "gvec", axis=1, tiled=True)
    mirrored = jnp.stack([gathered[0].T, -gathered[1].T])
    return (kernel_rows, mirrored)


def solution(mesh):
    placed = (P(None, "trans", "gvec"), P("gvec"), P("rows"))
    return jax.shard_map(
        body,
        mesh=mesh,
        in_specs=placed,
        out_specs=(P(None, ("rows", "gvec"), "trans"), P(None, "trans", "rows")),
        check_vma=False,
    )
```

profile of v0, /device:TPU:14, one launch (start us, length us, event | category | flops | bytes accessed | tf_op | source)
XLA Modules:
  0.0 407.7 jit_solution(2443535439191911137)
XLA Ops:
  7.2 0.0 all-reduce.2.cloned.1.call-start
  7.9 1.5 broadcast_select_fusion
  9.3 0.0 copy-start.1
  9.3 0.0 all-reduce.2.cloned.1.call-update
  9.4 0.0 copy-start
  9.4 0.0 reduce-scatter.2.cloned.1.call-start
  9.4 180.6 %all-reduce.2.cloned.1.call-done = bf16[2,1024,512]{2,1,0:T(8,128)(2,1)} async-done(((bf16[2,1024,512]{2,1,0:T(8,128)(2,1)}), bf16[2,1024,512]{2,1,0:T(8,128)(2,1)}) %all-reduce.2.cloned.1.call-update) | async-done | bytes 2097168 | tf_op jit(solution)/shard_map/psum | solution.py:9
  190.0 0.0 copy-done.1
  190.0 2.0 multiply_convert_fusion
  192.0 0.0 copy-done
  192.0 1.3 fusion.3
  193.3 1.3 fusion.7
  194.6 1.3 fusion.2
  195.9 1.3 fusion.1
  197.2 2.4 pad_maximum_fusion
  199.5 0.0 reduce-scatter.2.cloned.1.call-update
  199.6 0.0 all-gather.2.cloned.1.call-start
  199.6 94.9 %reduce-scatter.2.cloned.1.call-done = bf16[2,128,1024]{2,1,0:T(8,128)(2,1)} async-done(((bf16[2,1024,1024]{2,1,0:T(8,128)(2,1)}), bf16[2,128,1024]{2,1,0:T(8,128)(2,1)}) %reduce-scatter.2.cloned.1.call-update) | async-done | bytes 524304 | tf_op jit(solution)/shard_map/reduce_scatter | solution.py:24
  294.5 0.0 all-gather.2.cloned.1.call-update
  294.5 95.7 %all-gather.2.cloned.1.call-done = bf16[2,1024,1024]{2,1,0:T(8,128)(2,1)} async-done(((bf16[2,128,1024]{2,1,0:T(8,128)(2,1)}), bf16[2,1024,1024]{2,1,0:T(8,128)(2,1)}) %all-gather.2.cloned.1.call-update) | async-done | bytes 4194320 | tf_op jit(solution)/shard_map/all_gather | solution.py:27
  390.2 2.5 slice_bitcast_fusion
  392.7 2.3 pad_maximum_fusion.1
  395.0 6.2 %copy.5 = bf16[2,1024,1024]{2,1,0:T(8,128)(2,1)} copy(bf16[2,1024,1024]{1,2,0:T(8,128)(2,1)} %pad_maximum_fusion.1) | data formatting | bytes 8388608
Async XLA Ops:
  7.2 182.8 %all-reduce.2.cloned.1.call-start = ((), (), s32[]{:S(2)}) async-start(), calls=%async_computation.1 | async-start | bytes 4194304 | tf_op jit(solution)/shard_map/psum | solution.py:9
  9.3 180.6 %copy-start.1 = (f32[512]{0:T(512)S(1)}, f32[512]{0:T(512)}, u32[]{:S(2)}) copy-start(f32[512]{0:T(512)} %param.4) | copy-start | bytes 6148
  9.4 182.6 %copy-start = (bf16[2,1024,512]{2,1,0:T(8,128)(2,1)S(1)}, bf16[2,1024,512]{2,1,0:T(8,128)(2,1)}, u32[]{:S(2)}) copy-start(bf16[2,1024,512]{2,1,0:T(8,128)(2,1)} %param.3) | copy-start | bytes 6291460
  9.4 285.1 %reduce-scatter.2.cloned.1.call-start = ((), (), s32[]{:S(2)}) async-start(), calls=%async_computation.2 | async-start | bytes 4718592 | tf_op jit(solution)/shard_map/reduce_scatter | solution.py:24
  199.6 190.6 %all-gather.2.cloned.1.call-start = ((), (), s32[]{:S(2)}) async-start(), calls=%async_computation.3 | async-start | bytes 4718592 | tf_op jit(solution)/shard_map/all_gather | solution.py:27
Sparse Core Ops, SparseCore 0:
  11.2 178.7 all-reduce.1
  199.7 94.7 reduce-scatter.1
  296.8 93.2 all-gather.1
where the time goes:
time: 410 us; the launch traced here: 408 us
  waiting for transfers between devices  371 us (90%)
  between operations  14.4 us (4%)
  other arithmetic  10.6 us (3%)
  local copies, waits for them, and re-layouts  6.2 us (2%)
  matrix products  5.16 us (1%)
    psum x1, waiting for transfers between devices, from_root(): return lax.psum(kept, axis)  181 us
    all_gather x1, waiting for transfers between devices, body(): gathered = lax.all_gather(kernel_rows, 'gvec', axis=1, tiled=True)  95.7 us
    reduce_scatter x1, waiting for transfers between devices, body(): lax.psum_scatter(partial_terms.astype(jnp.bfloat16), 'gvec', scatter_dime...  94.9 us
  transfers between devices with their start and end apart: 3, of which 3 were waited for; matrix products, arithmetic and copies ran while one was open for 0% of the time, Pallas kernels for 0%

commit v1 on v0

v1 whole, which is shorter than its diff:
```python
import functools

import jax
import jax.numpy as jnp
from jax import lax
from jax.experimental import pallas as pl
from jax.experimental.pallas import tpu as pltpu
from jax.sharding import PartitionSpec as P

BF16 = jnp.bfloat16
F32 = jnp.float32
X_GROUPS = [[4 * x + z for x in range(4)] for z in range(4)]
ZY_GROUPS = [
    [8 * (4 * x + z) + 2 * y + p for z in range(4) for y in range(4)]
    for x in range(4)
    for p in range(2)
]
PAIR = [(2 * y + p, 2 * y + 1 - p) for y in range(4) for p in range(2)]
CORE = [(0, 1), (1, 0)]
LIMIT = 48 * 1024 * 1024


def along_x(step):
    return [(4 * x + z, 4 * ((x + step) % 4) + z) for x in range(4) for z in range(4)]


def along_z(step):
    return [(4 * x + z, 4 * x + (z + step) % 4) for x in range(4) for z in range(4)]


def along_y(step):
    return [(2 * y + p, 2 * ((y + step) % 4) + p) for y in range(4) for p in range(2)]


def send(value, axis, pairs):
    return lax.ppermute(value, axis, pairs)


def pick(value, index, axis):
    return lax.dynamic_index_in_dim(value, index, axis, keepdims=False)


def from_below(value, axis, pairs):
    one, three = send(value, axis, pairs(1)), send(value, axis, pairs(3))
    return one, send(value, axis, pairs(2)), three


def multiply_kernel(count, place_ref, *refs):
    chunks, right, out_ref = refs[:count], refs[count:-1], refs[-1]
    y, sign = place_ref[0], place_ref[1].astype(F32)
    for i, chunk_ref in enumerate(chunks):
        sums = []
        for component in range(2):
            total = None
            for d in range(4):
                left = chunk_ref[lax.rem(y + 4 - d, 4)].reshape(128, 512)
                term = lax.dot_general(
                    left,
                    right[4 * component + d][...],
                    (((1,), (1,)), ((), ())),
                    preferred_element_type=F32,
                )
                total = term if total is None else total + term
            sums.append(total)
        mine, twin = sums
        rows = pl.ds(64 * i, 64)
        out_ref[0, rows, :] = (mine[:64] + twin[64:]).astype(BF16)
        out_ref[1, rows, :] = (sign * (twin[:64] - mine[64:])).astype(BF16)


def multiply(place, chunks, right):
    count = len(chunks)
    return pl.pallas_call(
        functools.partial(multiply_kernel, count),
        grid_spec=pltpu.PrefetchScalarGridSpec(
            num_scalar_prefetch=1,
            grid=(4,),
            in_specs=[pl.BlockSpec((4, 2, 64, 512), lambda t, s: (0, 0, 0, 0))] * count
            + [pl.BlockSpec((256, 512), lambda t, s: (t, 0))] * 8,
            out_specs=pl.BlockSpec((2, 64 * count, 256), lambda t, s: (0, 0, t)),
        ),
        out_shape=jax.ShapeDtypeStruct((2, 64 * count, 1024), BF16),
        compiler_params=pltpu.CompilerParams(vmem_limit_bytes=LIMIT),
        cost_estimate=pl.CostEstimate(
            flops=count * 2**30, bytes_accessed=9 * 2**20, transcendentals=0
        ),
    )(place, *chunks, *right)


def place_rows(ref, start, value_ref, first, z):
    for k in range(4):
        to = pl.multiple_of(start + 16 * lax.rem(z + 4 - k, 4), 16)
        ref[pl.ds(to, 16), :] = value_ref[0, pl.ds(first + 16 * k, 16), :]


def place_chunks(ref, refs, x, z):
    own, sides, across = refs
    place_rows(ref, 64 * x, own, 0, z)
    place_rows(ref, 64 * lax.rem(x + 3, 4), sides, 0, z)
    place_rows(ref, 64 * lax.rem(x + 1, 4), sides, 64, z)
    place_rows(ref, 64 * lax.rem(x + 2, 4), across, 0, z)


def mirror_kernel(place_ref, *refs):
    pieces, out_ref, scratch = refs[:12], refs[12], refs[13]
    y, x, z = place_ref[0], place_ref[2], place_ref[3]
    sign = jnp.where(pl.program_id(0) == 0, 1.0, -1.0).astype(F32)
    for d in range(4):
        held = scratch.at[d]
        place_chunks(held, pieces[3 * d : 3 * d + 3], x, z)
        columns = pl.ds(pl.multiple_of(256 * lax.rem(y + 4 - d, 4), 256), 256)
        out_ref[0, :, columns] = (held[...].astype(F32) * sign).T.astype(BF16)


def piece_specs(width):
    return [
        pl.BlockSpec((1, rows, width), lambda c, t, s: (c, 0, t)) for rows in (64, 128, 64)
    ]


def mirror(place, pieces):
    return pl.pallas_call(
        mirror_kernel,
        grid_spec=pltpu.PrefetchScalarGridSpec(
            num_scalar_prefetch=1,
            grid=(2, 4),
            in_specs=piece_specs(256) * 4,
            out_specs=pl.BlockSpec((1, 256, 1024), lambda c, t, s: (c, t, 0)),
            scratch_shapes=[pltpu.VMEM((4, 256, 256), BF16)],
        ),
        out_shape=jax.ShapeDtypeStruct((2, 1024, 1024), BF16),
        compiler_params=pltpu.CompilerParams(vmem_limit_bytes=LIMIT),
        cost_estimate=pl.CostEstimate(flops=0, bytes_accessed=8 * 2**20, transcendentals=0),
    )(place, *pieces)


def rows_kernel(place_ref, own, sides, across, out_ref, scratch):
    x, z, p = place_ref[2], place_ref[3], place_ref[4]
    place_chunks(scratch, (own, sides, across), x, z)
    out_ref[0] = scratch[pl.ds(pl.multiple_of(128 * p, 128), 128), :]


def own_rows(place, pieces):
    return pl.pallas_call(
        rows_kernel,
        grid_spec=pltpu.PrefetchScalarGridSpec(
            num_scalar_prefetch=1,
            grid=(2, 1),
            in_specs=piece_specs(1024),
            out_specs=pl.BlockSpec((1, 128, 1024), lambda c, t, s: (c, 0, t)),
            scratch_shapes=[pltpu.VMEM((256, 1024), BF16)],
        ),
        out_shape=jax.ShapeDtypeStruct((2, 128, 1024), BF16),
        compiler_params=pltpu.CompilerParams(vmem_limit_bytes=LIMIT),
        cost_estimate=pl.CostEstimate(flops=0, bytes_accessed=3 * 2**19, transcendentals=0),
    )(place, *pieces)


def body(pair_density, coulomb, block_index):
    core = lax.axis_index("rows")
    trans = lax.axis_index("trans")
    gvec = lax.axis_index("gvec")
    x, z = trans // 4, trans % 4
    y, p = gvec // 2, gvec % 2
    place = jnp.stack([y, 1 - 2 * core, x, z, p]).astype(jnp.int32)
    block = block_index[0]
    other_block = send(block_index, "rows", CORE)[0]

    mine = pick(pair_density, core, 0)
    gathered = from_below(mine, "gvec", along_y)
    twin = pick(pair_density, 1 - core, 0)
    right = [mine, *gathered, twin, *(send(value, "rows", CORE) for value in gathered)]

    parts = mine.reshape(4, 4, 64, 512).transpose(1, 0, 2, 3)
    got = lax.all_to_all(parts, "trans", 0, 0, axis_index_groups=X_GROUPS, tiled=True)
    swapped = send(pick(got, other_block // 4, 0), "rows", CORE)
    share = jnp.stack([pick(got, block // 4, 0), swapped], axis=1)
    share = (share.astype(F32) * coulomb).astype(BF16)
    share = share.reshape(4, 2, 4, 16, 512).transpose(2, 0, 1, 3, 4).reshape(16, 2, 16, 512)
    got = lax.all_to_all(
        share, ("trans", "gvec"), 0, 0, axis_index_groups=ZY_GROUPS, tiled=True
    )
    share = pick(got.reshape(4, 4, 2, 16, 512), block % 4, 0)
    chunk = jnp.concatenate([share, *from_below(share, "trans", along_z)], axis=2)
    below, across, above = from_below(chunk, "trans", along_x)

    pieces = []
    for chunks in ((chunk,), (below, above), (across,)):
        partial_terms = multiply(place, chunks, right)
        coming = send(partial_terms, "gvec", PAIR)
        summed = (partial_terms.astype(F32) + coming.astype(F32)).astype(BF16)
        pieces.append((summed, *from_below(summed, "gvec", along_y)))
    kernel_rows = own_rows(place, [piece[0] for piece in pieces])
    mirrored = mirror(place, [piece[d] for d in range(4) for piece in pieces])
    return (kernel_rows, mirrored)


def solution(mesh):
    placed = (P(None, "trans", "gvec"), P("gvec"), P("rows"))
    return jax.shard_map(
        body,
        mesh=mesh,
        in_specs=placed,
        out_specs=(P(None, ("rows", "gvec"), "trans"), P(None, "trans", "rows")),
        check_vma=False,
    )
```

time: 410 us -> 193 us (0.47)
  waiting for transfers between devices: 371 us -> 105 us
  starting transfers between devices: 0.12 us -> 50.2 us
  Pallas kernels: 0 us -> 27.6 us
  between operations: 14.4 us -> 4.02 us
  other arithmetic: 10.6 us -> 1.28 us
  matrix products: 5.16 us -> 0 us
    psum x1 -> x0, waiting for transfers between devices: 181 us -> none  [from_root(): return lax.psum(kept, axis)]
    all_gather x1 -> x0, waiting for transfers between devices: 95.7 us -> none  [body(): gathered = lax.all_gather(kernel_rows, 'gvec', axis=1, tiled=True)]
    reduce_scatter x1 -> x0, waiting for transfers between devices: 94.9 us -> none  [body(): lax.psum_scatter(partial_terms.astype(jnp.bfloat16), 'gvec', scatter_dime...]
    ppermute x0 -> x26, waiting for transfers between devices: none -> 93.1 us  [send(): return lax.ppermute(value, axis, pairs)]
    ppermute x0 -> x26, starting transfers between devices: none -> 35.4 us  [send(): return lax.ppermute(value, axis, pairs)]
    pallas_call x0 -> x5, Pallas kernels: none -> 27.6 us  [the longest x3 20.5 us: multiply(): pl.pallas_call(functools.partial(multiply_kernel, count), grid_spec=pltpu...]
    all_to_all x0 -> x2, starting transfers between devices: none -> 14.8 us  [the longest x1 9.94 us: body(): lax.all_to_all(share, ('trans', 'gvec'), 0, 0, axis_index_groups=ZY_GROUP...]
    all_to_all x0 -> x2, waiting for transfers between devices: none -> 11.4 us  [the longest x1 9.24 us: body(): lax.all_to_all(parts, 'trans', 0, 0, axis_index_groups=X_GROUPS, tiled=True)]
  transfers between devices with their start and end apart: 3 -> 28, of which waited for: 3 -> 14; matrix products, arithmetic and copies ran while one was open for 0% -> 2% of each run, Pallas kernels for 0% -> 11%
where the time goes in v1:
time: 193 us; the launch traced here: 192 us
  waiting for transfers between devices  105 us (54%)
  starting transfers between devices  50.2 us (26%)
  Pallas kernels  27.6 us (14%)
  local copies, waits for them, and re-layouts  4.72 us (2%)
  between operations  4.02 us (2%)
    ppermute x26, waiting for transfers between devices, send(): return lax.ppermute(value, axis, pairs)  93.1 us
    ppermute x26, starting transfers between devices, send(): return lax.ppermute(value, axis, pairs)  35.4 us
    pallas_call x3, Pallas kernels, multiply(): pl.pallas_call(functools.partial(multiply_kernel, count), grid_spec=pltpu...  20.5 us
    all_to_all x1, starting transfers between devices, body(): lax.all_to_all(share, ('trans', 'gvec'), 0, 0, axis_index_groups=ZY_GROUP...  9.94 us
    all_to_all x1, waiting for transfers between devices, body(): lax.all_to_all(parts, 'trans', 0, 0, axis_index_groups=X_GROUPS, tiled=True)  9.24 us
    pallas_call x1, Pallas kernels, mirror(): pl.pallas_call(mirror_kernel, grid_spec=pltpu.PrefetchScalarGridSpec(num_...  5.68 us
    all_to_all x1, starting transfers between devices, body(): lax.all_to_all(parts, 'trans', 0, 0, axis_index_groups=X_GROUPS, tiled=True)  4.9 us
  transfers between devices with their start and end apart: 28, of which 14 were waited for; matrix products, arithmetic and copies ran while one was open for 2% of the time, Pallas kernels for 11%

profile of v1, /device:TPU:14, one launch (start us, length us, event | category | flops | bytes accessed | tf_op | source)
XLA Modules:
  0.0 192.3 jit_solution(7612710321167544816)
XLA Ops:
  0.6 1.7 dynamic-slice_bitcast_fusion
  2.3 1.2 copy.6
  3.5 4.9 %all-to-all-start = ((bf16[4,4,64,512]{3,2,1,0:T(8,128)(2,1)}), bf16[4,4,64,512]{3,2,1,0:T(8,128)(2,1)S(1)}, u32[]{:S(2)}, u32[]{:S(2)}) async-start(bf16[4,4,64,512]{3,2,1,0:T(8,128)(2,1)} %copy.6), calls=%async_computation | async-start | bytes 2097152 | tf_op jit(solution)/shard_map/all_to_all | solution.py:175
  8.4 0.0 collective-permute-start
  9.1 0.6 collective-permute-done
  12.2 9.2 %all-to-all-done = bf16[4,4,64,512]{3,2,1,0:T(8,128)(2,1)S(1)} async-done(((bf16[4,4,64,512]{3,2,1,0:T(8,128)(2,1)}), bf16[4,4,64,512]{3,2,1,0:T(8,128)(2,1)S(1)}, u32[]{:S(2)}, u32[]{:S(2)}) %all-to-all-start) | async-done | bytes 1048608 | tf_op jit(solution)/shard_map/all_to_all | solution.py:175
  21.5 0.1 collective-permute-start.1
  21.6 1.7 collective-permute-start.5
  23.2 0.9 collective-permute-start.6
  24.2 2.4 %collective-permute-start.7 = (bf16[1024,512]{1,0:T(8,128)(2,1)S(1)}, bf16[1024,512]{1,0:T(8,128)(2,1)}, u32[]{:S(2)}, u32[]{:S(2)}) collective-permute-start(bf16[1024,512]{1,0:T(8,128)(2,1)S(1)} %bitcast.30), channel_id=1, source_target_pairs={{0,6},{1,7},{2,0},{3,1},{4,2},{5,3},{6,4},{7,5},{8,14},{9,15},{10,... | collective-permute-start | bytes 3145736 | tf_op jit(solution)/shard_map/ppermute | solution.py:36
  26.6 0.0 collective-permute-done.1
  26.6 0.1 fusion
  26.7 0.8 copy.7
  27.5 9.9 %all-to-all-start.1 = ((bf16[16,2,16,512]{3,2,1,0:T(8,128)(2,1)}), bf16[16,2,16,512]{3,2,1,0:T(8,128)(2,1)}, u32[]{:S(2)}, u32[]{:S(2)}) async-start(bf16[16,2,16,512]{3,2,1,0:T(8,128)(2,1)} %bitcast.34), calls=%async_computation.1 | async-start | bytes 1048576 | tf_op jit(solution)/shard_map/all_to_all | solution.py:180
  37.5 14.2 %collective-permute-done.5.refs_2_.refs_3_ = bf16[1024,512]{1,0:T(8,128)(2,1)S(1)} collective-permute-done((bf16[1024,512]{1,0:T(8,128)(2,1)S(1)}, bf16[1024,512]{1,0:T(8,128)(2,1)S(1)}, u32[]{:S(2)}, u32[]{:S(2)}) %collective-permute-start.5) | collective-permute-done | bytes 1048608 | tf_op jit(solution)/shard_map/ppermute | solution.py:36
  51.7 0.0 collective-permute-start.8
  51.7 4.1 %collective-permute-done.6.refs_3_.refs_4_ = bf16[1024,512]{1,0:T(8,128)(2,1)} collective-permute-done((bf16[1024,512]{1,0:T(8,128)(2,1)S(1)}, bf16[1024,512]{1,0:T(8,128)(2,1)}, u32[]{:S(2)}, u32[]{:S(2)}) %collective-permute-start.6) | collective-permute-done | bytes 1048608 | tf_op jit(solution)/shard_map/ppermute | solution.py:36
  55.7 0.0 collective-permute-start.9
  55.7 20.5 %collective-permute-done.7.refs_4_.refs_5_ = bf16[1024,512]{1,0:T(8,128)(2,1)} collective-permute-done((bf16[1024,512]{1,0:T(8,128)(2,1)S(1)}, bf16[1024,512]{1,0:T(8,128)(2,1)}, u32[]{:S(2)}, u32[]{:S(2)}) %collective-permute-start.7) | collective-permute-done | bytes 1048608 | tf_op jit(solution)/shard_map/ppermute | solution.py:36
  76.3 0.0 collective-permute-start.10
  76.3 2.2 %all-to-all-done.1 = bf16[16,2,16,512]{3,2,1,0:T(8,128)(2,1)} async-done(((bf16[16,2,16,512]{3,2,1,0:T(8,128)(2,1)}), bf16[16,2,16,512]{3,2,1,0:T(8,128)(2,1)}, u32[]{:S(2)}, u32[]{:S(2)}) %all-to-all-start.1) | async-done | bytes 524320 | tf_op jit(solution)/shard_map/all_to_all | solution.py:180
  78.5 0.9 dynamic-slice_bitcast_fusion.2
  79.4 6.2 %collective-permute-start.4 = (bf16[4,2,16,512]{3,2,1,0:T(8,128)(2,1)S(1)}, bf16[4,2,16,512]{3,2,1,0:T(8,128)(2,1)S(1)}, u32[]{:S(2)}, u32[]{:S(2)}) collective-permute-start(bf16[4,2,16,512]{3,2,1,0:T(8,128)(2,1)S(1)} %dynamic-slice_bitcast_fusion.2), channel_id=1, source_target_pairs={{0,24},{8,0},{16,8},{24,16},{32,56},{40,32},{48,40},{56,48},{64,88... | collective-permute-start | bytes 393224 | tf_op jit(solution)/shard_map/ppermute | solution.py:36
  85.5 1.2 collective-permute-start.3
  86.8 8.8 %collective-permute-done.4 = bf16[4,2,16,512]{3,2,1,0:T(8,128)(2,1)S(1)} collective-permute-done((bf16[4,2,16,512]{3,2,1,0:T(8,128)(2,1)S(1)}, bf16[4,2,16,512]{3,2,1,0:T(8,128)(2,1)S(1)}, u32[]{:S(2)}, u32[]{:S(2)}) %collective-permute-start.4) | collective-permute-done | bytes 131104 | tf_op jit(solution)/shard_map/ppermute | solution.py:36
  95.6 0.0 collective-permute-start.2
  95.6 0.3 collective-permute-done.3
  95.9 7.2 %collective-permute-done.2 = bf16[4,2,16,512]{3,2,1,0:T(8,128)(2,1)S(1)} collective-permute-done((bf16[4,2,16,512]{3,2,1,0:T(8,128)(2,1)S(1)}, bf16[4,2,16,512]{3,2,1,0:T(8,128)(2,1)S(1)}, u32[]{:S(2)}, u32[]{:S(2)}) %collective-permute-start.2) | collective-permute-done | bytes 131104 | tf_op jit(solution)/shard_map/ppermute | solution.py:36
  103.1 0.8 pad_maximum_fusion.refs_0_
  103.9 2.1 %collective-permute-start.12 = (bf16[4,2,64,512]{3,2,1,0:T(8,128)(2,1)}, bf16[4,2,64,512]{3,2,1,0:T(8,128)(2,1)}, u32[]{:S(2)}, u32[]{:S(2)}) collective-permute-start(bf16[4,2,64,512]{3,2,1,0:T(8,128)(2,1)} %pad_maximum_fusion.refs_0_), channel_id=1, source_target_pairs={{0,32},{8,40},{16,48},{24,56},{32,64},{40,72},{48,80},{56,88},{64,... | collective-permute-start | bytes 1572872 | tf_op jit(solution)/shard_map/ppermute | solution.py:36
  106.0 0.0 collective-permute-start.13
  106.0 0.0 collective-permute-done.8.refs_6_.refs_7_
  106.0 2.0 %collective-permute-start.15 = (bf16[4,2,64,512]{3,2,1,0:T(8,128)(2,1)}, bf16[4,2,64,512]{3,2,1,0:T(8,128)(2,1)}, u32[]{:S(2)}, u32[]{:S(2)}) collective-permute-start(bf16[4,2,64,512]{3,2,1,0:T(8,128)(2,1)} %pad_maximum_fusion.refs_0_), channel_id=1, source_target_pairs={{0,64},{8,72},{16,80},{24,88},{32,96},{40,104},{48,112},{56,120},{... | collective-permute-start | bytes 1572872 | tf_op jit(solution)/shard_map/ppermute | solution.py:36
  108.0 0.1 stack.32.place_ref
  108.1 0.0 collective-permute-done.9.refs_7_.refs_8_
  108.1 0.0 collective-permute-done.10.refs_8_.refs_9_
  108.1 6.0 %shard_map.50 = bf16[2,64,1024]{2,1,0:T(8,128)(2,1)S(1)} custom-call(s32[5]{0:T(128)S(1)} %stack.32.place_ref, bf16[4,2,64,512]{3,2,1,0:T(8,128)(2,1)} %pad_maximum_fusion.refs_0_, bf16[1024,512]{1,0:T(8,128)(2,1)S(1)} %bitcast.31, bf16[1024,512]{1,0:T(8,128)(2,1)S(1)} %collective-permute-done.5.refs_2_.refs_3_, ...), custom_call_target="tpu_custom_call" | custom-call | flops 1073741824 | bytes 9437184 | tf_op jit(solution)/shard_map/pallas_call | solution.py:73
  114.2 0.1 collective-permute-start.11
  114.3 13.0 %collective-permute-done.12.refs_0_ = bf16[4,2,64,512]{3,2,1,0:T(8,128)(2,1)} collective-permute-done((bf16[4,2,64,512]{3,2,1,0:T(8,128)(2,1)}, bf16[4,2,64,512]{3,2,1,0:T(8,128)(2,1)}, u32[]{:S(2)}, u32[]{:S(2)}) %collective-permute-start.12) | collective-permute-done | bytes 524320 | tf_op jit(solution)/shard_map/ppermute | solution.py:36
  127.3 3.4 %collective-permute-done.13.refs_1_ = bf16[4,2,64,512]{3,2,1,0:T(8,128)(2,1)} collective-permute-done((bf16[4,2,64,512]{3,2,1,0:T(8,128)(2,1)}, bf16[4,2,64,512]{3,2,1,0:T(8,128)(2,1)}, u32[]{:S(2)}, u32[]{:S(2)}) %collective-permute-start.13) | collective-permute-done | bytes 524320 | tf_op jit(solution)/shard_map/ppermute | solution.py:36
  130.7 8.4 %shard_map.51 = bf16[2,128,1024]{2,1,0:T(8,128)(2,1)S(1)} custom-call(s32[5]{0:T(128)S(1)} %stack.32.place_ref, bf16[4,2,64,512]{3,2,1,0:T(8,128)(2,1)} %collective-permute-done.12.refs_0_, bf16[4,2,64,512]{3,2,1,0:T(8,128)(2,1)} %collective-permute-done.13.refs_1_, bf16[1024,512]{1,0:T(8,128)(2,1)S(1)} %bitcast.32, ...), custom_call_target="tpu_custom_call" | custom-call | flops 2147483648 | bytes 9437184 | tf_op jit(solution)/shard_map/pallas_call | solution.py:73
  139.1 0.3 collective-permute-start.14
  139.4 6.0 %shard_map.52 = bf16[2,64,1024]{2,1,0:T(8,128)(2,1)S(1)} custom-call(s32[5]{0:T(128)S(1)} %stack.32.place_ref, bf16[4,2,64,512]{3,2,1,0:T(8,128)(2,1)} %collective-permute-done.15.refs_0_, bf16[1024,512]{1,0:T(8,128)(2,1)S(1)} %bitcast.33, bf16[1024,512]{1,0:T(8,128)(2,1)S(1)} %collective-permute-done.5.refs_2_.refs_3_, ...), custom_call_target="tpu_custom_call" | custom-call | flops 1073741824 | bytes 9437184 | tf_op jit(solution)/shard_map/pallas_call | solution.py:73
  145.5 2.1 %collective-permute-start.16 = (bf16[2,64,1024]{2,1,0:T(8,128)(2,1)S(1)}, bf16[2,64,1024]{2,1,0:T(8,128)(2,1)S(1)}, u32[]{:S(2)}, u32[]{:S(2)}) collective-permute-start(bf16[2,64,1024]{2,1,0:T(8,128)(2,1)S(1)} %shard_map.52), channel_id=1, source_target_pairs={{0,1},{1,0},{2,3},{3,2},{4,5},{5,4},{6,7},{7,6},{8,9},{9,8},{10,11... | collective-permute-start | bytes 786440 | tf_op jit(solution)/shard_map/ppermute | solution.py:36
  147.6 0.1 add_convert_fusion.2.own.refs_0_
  147.6 2.7 %collective-permute-start.17 = (bf16[2,64,1024]{2,1,0:T(8,128)(2,1)S(1)}, bf16[2,64,1024]{2,1,0:T(8,128)(2,1)S(1)}, u32[]{:S(2)}, u32[]{:S(2)}) collective-permute-start(bf16[2,64,1024]{2,1,0:T(8,128)(2,1)S(1)} %add_convert_fusion.2.own.refs_0_), channel_id=1, source_target_pairs={{0,2},{1,3},{2,4},{3,5},{4,6},{5,7},{6,0},{7,1},{8,10},{9,11},{10,... | collective-permute-start | bytes 786440 | tf_op jit(solution)/shard_map/ppermute | solution.py:36
  150.3 1.5 collective-permute-start.20
  151.8 0.7 collective-permute-start.23
  152.5 0.0 collective-permute-done.16
  152.5 0.1 add_convert_fusion.1.across.refs_2_
  152.6 2.1 %collective-permute-start.19 = (bf16[2,64,1024]{2,1,0:T(8,128)(2,1)S(1)}, bf16[2,64,1024]{2,1,0:T(8,128)(2,1)S(1)}, u32[]{:S(2)}, u32[]{:S(2)}) collective-permute-start(bf16[2,64,1024]{2,1,0:T(8,128)(2,1)S(1)} %add_convert_fusion.1.across.refs_2_), channel_id=1, source_target_pairs={{0,2},{1,3},{2,4},{3,5},{4,6},{5,7},{6,0},{7,1},{8,10},{9,11},{10,... | collective-permute-start | bytes 786440 | tf_op jit(solution)/shard_map/ppermute | solution.py:36
  154.7 0.2 add_convert_fusion.sides.refs_1_
  154.9 0.1 collective-permute-start.18
  155.0 7.5 %collective-permute-done.17.refs_3_ = bf16[2,64,1024]{2,1,0:T(8,128)(2,1)S(1)} collective-permute-done((bf16[2,64,1024]{2,1,0:T(8,128)(2,1)S(1)}, bf16[2,64,1024]{2,1,0:T(8,128)(2,1)S(1)}, u32[]{:S(2)}, u32[]{:S(2)}) %collective-permute-start.17) | collective-permute-done | bytes 262176 | tf_op jit(solution)/shard_map/ppermute | solution.py:36
  162.5 2.0 %collective-permute-start.21 = (bf16[2,128,1024]{2,1,0:T(8,128)(2,1)S(1)}, bf16[2,128,1024]{2,1,0:T(8,128)(2,1)S(1)}, u32[]{:S(2)}, u32[]{:S(2)}) collective-permute-start(bf16[2,128,1024]{2,1,0:T(8,128)(2,1)S(1)} %add_convert_fusion.sides.refs_1_), channel_id=1, source_target_pairs={{0,4},{1,5},{2,6},{3,7},{4,0},{5,1},{6,2},{7,3},{8,12},{9,13},{10,... | collective-permute-start | bytes 1572872 | tf_op jit(solution)/shard_map/ppermute | solution.py:36
  164.5 2.7 %collective-permute-start.24 = (bf16[2,128,1024]{2,1,0:T(8,128)(2,1)S(1)}, bf16[2,128,1024]{2,1,0:T(8,128)(2,1)S(1)}, u32[]{:S(2)}, u32[]{:S(2)}) collective-permute-start(bf16[2,128,1024]{2,1,0:T(8,128)(2,1)S(1)} %add_convert_fusion.sides.refs_1_), channel_id=1, source_target_pairs={{0,6},{1,7},{2,0},{3,1},{4,2},{5,3},{6,4},{7,5},{8,14},{9,15},{10,... | collective-permute-start | bytes 1572872 | tf_op jit(solution)/shard_map/ppermute | solution.py:36
  167.2 0.0 collective-permute-done.23.refs_9_
  167.2 2.0 %collective-permute-start.22 = (bf16[2,64,1024]{2,1,0:T(8,128)(2,1)S(1)}, bf16[2,64,1024]{2,1,0:T(8,128)(2,1)S(1)}, u32[]{:S(2)}, u32[]{:S(2)}) collective-permute-start(bf16[2,64,1024]{2,1,0:T(8,128)(2,1)S(1)} %add_convert_fusion.1.across.refs_2_), channel_id=1, source_target_pairs={{0,4},{1,5},{2,6},{3,7},{4,0},{5,1},{6,2},{7,3},{8,12},{9,13},{10,... | collective-permute-start | bytes 786440 | tf_op jit(solution)/shard_map/ppermute | solution.py:36
  169.2 0.0 collective-permute-done.19.refs_5_
  169.2 2.6 %collective-permute-start.25 = (bf16[2,64,1024]{2,1,0:T(8,128)(2,1)S(1)}, bf16[2,64,1024]{2,1,0:T(8,128)(2,1)S(1)}, u32[]{:S(2)}, u32[]{:S(2)}) collective-permute-start(bf16[2,64,1024]{2,1,0:T(8,128)(2,1)S(1)} %add_convert_fusion.1.across.refs_2_), channel_id=1, source_target_pairs={{0,6},{1,7},{2,0},{3,1},{4,2},{5,3},{6,4},{7,5},{8,14},{9,15},{10,... | collective-permute-start | bytes 786440 | tf_op jit(solution)/shard_map/ppermute | solution.py:36
  171.7 1.4 shard_map.53
  173.2 10.8 %collective-permute-done.22.refs_8_ = bf16[2,64,1024]{2,1,0:T(8,128)(2,1)S(1)} collective-permute-done((bf16[2,64,1024]{2,1,0:T(8,128)(2,1)S(1)}, bf16[2,64,1024]{2,1,0:T(8,128)(2,1)S(1)}, u32[]{:S(2)}, u32[]{:S(2)}) %collective-permute-start.22) | collective-permute-done | bytes 262176 | tf_op jit(solution)/shard_map/ppermute | solution.py:36
  184.0 2.6 %collective-permute-done.25.refs_11_ = bf16[2,64,1024]{2,1,0:T(8,128)(2,1)S(1)} collective-permute-done((bf16[2,64,1024]{2,1,0:T(8,128)(2,1)S(1)}, bf16[2,64,1024]{2,1,0:T(8,128)(2,1)S(1)}, u32[]{:S(2)}, u32[]{:S(2)}) %collective-permute-start.25) | collective-permute-done | bytes 262176 | tf_op jit(solution)/shard_map/ppermute | solution.py:36
  186.6 5.7 %shard_map.54 = bf16[2,1024,1024]{2,1,0:T(8,128)(2,1)} custom-call(s32[5]{0:T(128)S(1)} %stack.32.place_ref, bf16[2,64,1024]{2,1,0:T(8,128)(2,1)S(1)} %add_convert_fusion.2.own.refs_0_, bf16[2,128,1024]{2,1,0:T(8,128)(2,1)S(1)} %add_convert_fusion.sides.refs_1_, bf16[2,64,1024]{2,1,0:T(8,128)(2,1)S(1)} %add_convert_fusion.1.across.refs_2_, ...), custom_call_target="tpu_custom_call" | custom-call | bytes 8388608 | tf_op jit(solution)/shard_map/pallas_call | solution.py:122
  (14 shorter events, 0.1 us)
Async XLA Ops:
  2.3 105.8 %copy-start = (bf16[1024,512]{1,0:T(8,128)(2,1)}, bf16[1024,512]{1,0:T(8,128)(2,1)S(1)}, u32[]{:S(2)}) copy-start(bf16[1024,512]{1,0:T(8,128)(2,1)S(1)} %get-tuple-element.2.refs_5_.refs_6_) | copy-start | bytes 3145732
  3.5 23.1 %copy-start.2 = (f32[512]{0:T(512)S(1)}, f32[512]{0:T(512)}, u32[]{:S(2)}) copy-start(f32[512]{0:T(512)} %param.4) | copy-start | bytes 6148
  3.5 17.9 %all-to-all-start = ((bf16[4,4,64,512]{3,2,1,0:T(8,128)(2,1)}), bf16[4,4,64,512]{3,2,1,0:T(8,128)(2,1)S(1)}, u32[]{:S(2)}, u32[]{:S(2)}) async-start(bf16[4,4,64,512]{3,2,1,0:T(8,128)(2,1)} %copy.6), calls=%async_computation | async-start | bytes 2097152 | tf_op jit(solution)/shard_map/all_to_all | solution.py:175
  8.4 1.2 collective-permute-start
  21.5 5.1 %collective-permute-start.1 = (bf16[4,64,512]{2,1,0:T(8,128)(2,1)S(1)}, bf16[4,64,512]{2,1,0:T(8,128)(2,1)S(1)}, u32[]{:S(2)}, u32[]{:S(2)}) collective-permute-start(bf16[4,64,512]{2,1,0:T(8,128)(2,1)S(1)} %get-tuple-element.5), channel_id=1, source_target_pairs={{0,128},{128,0},{1,129},{129,1},{2,130},{130,2},{3,131},{131,3},{4... | collective-permute-start | bytes 786440 | tf_op jit(solution)/shard_map/ppermute | solution.py:36
  21.6 30.1 %collective-permute-start.5 = (bf16[1024,512]{1,0:T(8,128)(2,1)S(1)}, bf16[1024,512]{1,0:T(8,128)(2,1)S(1)}, u32[]{:S(2)}, u32[]{:S(2)}) collective-permute-start(bf16[1024,512]{1,0:T(8,128)(2,1)S(1)} %bitcast.28), channel_id=1, source_target_pairs={{0,2},{1,3},{2,4},{3,5},{4,6},{5,7},{6,0},{7,1},{8,10},{9,11},{10,... | collective-permute-start | bytes 3145736 | tf_op jit(solution)/shard_map/ppermute | solution.py:36
  23.2 32.5 %collective-permute-start.6 = (bf16[1024,512]{1,0:T(8,128)(2,1)S(1)}, bf16[1024,512]{1,0:T(8,128)(2,1)}, u32[]{:S(2)}, u32[]{:S(2)}) collective-permute-start(bf16[1024,512]{1,0:T(8,128)(2,1)S(1)} %bitcast.29), channel_id=1, source_target_pairs={{0,4},{1,5},{2,6},{3,7},{4,0},{5,1},{6,2},{7,3},{8,12},{9,13},{10,... | collective-permute-start | bytes 3145736 | tf_op jit(solution)/shard_map/ppermute | solution.py:36
  24.2 52.1 %collective-permute-start.7 = (bf16[1024,512]{1,0:T(8,128)(2,1)S(1)}, bf16[1024,512]{1,0:T(8,128)(2,1)}, u32[]{:S(2)}, u32[]{:S(2)}) collective-permute-start(bf16[1024,512]{1,0:T(8,128)(2,1)S(1)} %bitcast.30), channel_id=1, source_target_pairs={{0,6},{1,7},{2,0},{3,1},{4,2},{5,3},{6,4},{7,5},{8,14},{9,15},{10,... | collective-permute-start | bytes 3145736 | tf_op jit(solution)/shard_map/ppermute | solution.py:36
  27.5 50.9 %all-to-all-start.1 = ((bf16[16,2,16,512]{3,2,1,0:T(8,128)(2,1)}), bf16[16,2,16,512]{3,2,1,0:T(8,128)(2,1)}, u32[]{:S(2)}, u32[]{:S(2)}) async-start(bf16[16,2,16,512]{3,2,1,0:T(8,128)(2,1)} %bitcast.34), calls=%async_computation.1 | async-start | bytes 1048576 | tf_op jit(solution)/shard_map/all_to_all | solution.py:180
  51.7 54.4 %collective-permute-start.8 = (bf16[1024,512]{1,0:T(8,128)(2,1)S(1)}, bf16[1024,512]{1,0:T(8,128)(2,1)}, u32[]{:S(2)}, u32[]{:S(2)}) collective-permute-start(bf16[1024,512]{1,0:T(8,128)(2,1)S(1)} %collective-permute-done.5.refs_2_.refs_3_), channel_id=1, source_target_pairs={{0,128},{128,0},{1,129},{129,1},{2,130},{130,2},{3,131},{131,3},{4... | collective-permute-start | bytes 3145736 | tf_op jit(solution)/shard_map/ppermute | solution.py:36
  55.7 52.4 %collective-permute-start.9 = (bf16[1024,512]{1,0:T(8,128)(2,1)}, bf16[1024,512]{1,0:T(8,128)(2,1)}, u32[]{:S(2)}, u32[]{:S(2)}) collective-permute-start(bf16[1024,512]{1,0:T(8,128)(2,1)} %collective-permute-done.6.refs_3_.refs_4_), channel_id=1, source_target_pairs={{0,128},{128,0},{1,129},{129,1},{2,130},{130,2},{3,131},{131,3},{4... | collective-permute-start | bytes 3145736 | tf_op jit(solution)/shard_map/ppermute | solution.py:36
  76.3 31.9 %collective-permute-start.10 = (bf16[1024,512]{1,0:T(8,128)(2,1)}, bf16[1024,512]{1,0:T(8,128)(2,1)}, u32[]{:S(2)}, u32[]{:S(2)}) collective-permute-start(bf16[1024,512]{1,0:T(8,128)(2,1)} %collective-permute-done.7.refs_4_.refs_5_), channel_id=1, source_target_pairs={{0,128},{128,0},{1,129},{129,1},{2,130},{130,2},{3,131},{131,3},{4... | collective-permute-start | bytes 3145736 | tf_op jit(solution)/shard_map/ppermute | solution.py:36
  79.4 16.2 %collective-permute-start.4 = (bf16[4,2,16,512]{3,2,1,0:T(8,128)(2,1)S(1)}, bf16[4,2,16,512]{3,2,1,0:T(8,128)(2,1)S(1)}, u32[]{:S(2)}, u32[]{:S(2)}) collective-permute-start(bf16[4,2,16,512]{3,2,1,0:T(8,128)(2,1)S(1)} %dynamic-slice_bitcast_fusion.2), channel_id=1, source_target_pairs={{0,24},{8,0},{16,8},{24,16},{32,56},{40,32},{48,40},{56,48},{64,88... | collective-permute-start | bytes 393224 | tf_op jit(solution)/shard_map/ppermute | solution.py:36
  85.5 10.4 %collective-permute-start.3 = (bf16[4,2,16,512]{3,2,1,0:T(8,128)(2,1)S(1)}, bf16[4,2,16,512]{3,2,1,0:T(8,128)(2,1)S(1)}, u32[]{:S(2)}, u32[]{:S(2)}) collective-permute-start(bf16[4,2,16,512]{3,2,1,0:T(8,128)(2,1)S(1)} %dynamic-slice_bitcast_fusion.2), channel_id=1, source_target_pairs={{0,16},{8,24},{16,0},{24,8},{32,48},{40,56},{48,32},{56,40},{64,80... | collective-permute-start | bytes 393224 | tf_op jit(solution)/shard_map/ppermute | solution.py:36
  95.6 7.5 %collective-permute-start.2 = (bf16[4,2,16,512]{3,2,1,0:T(8,128)(2,1)S(1)}, bf16[4,2,16,512]{3,2,1,0:T(8,128)(2,1)S(1)}, u32[]{:S(2)}, u32[]{:S(2)}) collective-permute-start(bf16[4,2,16,512]{3,2,1,0:T(8,128)(2,1)S(1)} %dynamic-slice_bitcast_fusion.2), channel_id=1, source_target_pairs={{0,8},{8,16},{16,24},{24,0},{32,40},{40,48},{48,56},{56,32},{64,72... | collective-permute-start | bytes 393224 | tf_op jit(solution)/shard_map/ppermute | solution.py:36
  103.9 23.4 %collective-permute-start.12 = (bf16[4,2,64,512]{3,2,1,0:T(8,128)(2,1)}, bf16[4,2,64,512]{3,2,1,0:T(8,128)(2,1)}, u32[]{:S(2)}, u32[]{:S(2)}) collective-permute-start(bf16[4,2,64,512]{3,2,1,0:T(8,128)(2,1)} %pad_maximum_fusion.refs_0_), channel_id=1, source_target_pairs={{0,32},{8,40},{16,48},{24,56},{32,64},{40,72},{48,80},{56,88},{64,... | collective-permute-start | bytes 1572872 | tf_op jit(solution)/shard_map/ppermute | solution.py:36
  106.0 24.7 %collective-permute-start.13 = (bf16[4,2,64,512]{3,2,1,0:T(8,128)(2,1)}, bf16[4,2,64,512]{3,2,1,0:T(8,128)(2,1)}, u32[]{:S(2)}, u32[]{:S(2)}) collective-permute-start(bf16[4,2,64,512]{3,2,1,0:T(8,128)(2,1)} %pad_maximum_fusion.refs_0_), channel_id=1, source_target_pairs={{0,96},{8,104},{16,112},{24,120},{32,0},{40,8},{48,16},{56,24},{64... | collective-permute-start | bytes 1572872 | tf_op jit(solution)/shard_map/ppermute | solution.py:36
  106.0 33.4 %collective-permute-start.15 = (bf16[4,2,64,512]{3,2,1,0:T(8,128)(2,1)}, bf16[4,2,64,512]{3,2,1,0:T(8,128)(2,1)}, u32[]{:S(2)}, u32[]{:S(2)}) collective-permute-start(bf16[4,2,64,512]{3,2,1,0:T(8,128)(2,1)} %pad_maximum_fusion.refs_0_), channel_id=1, source_target_pairs={{0,64},{8,72},{16,80},{24,88},{32,96},{40,104},{48,112},{56,120},{... | collective-permute-start | bytes 1572872 | tf_op jit(solution)/shard_map/ppermute | solution.py:36
  114.2 25.3 %copy-start.1 = (bf16[1024,512]{1,0:T(8,128)(2,1)S(1)}, bf16[1024,512]{1,0:T(8,128)(2,1)}, u32[]{:S(2)}) copy-start(bf16[1024,512]{1,0:T(8,128)(2,1)} %copy-done) | copy-start | bytes 3145732
  114.2 33.4 %collective-permute-start.11 = (bf16[2,64,1024]{2,1,0:T(8,128)(2,1)S(1)}, bf16[2,64,1024]{2,1,0:T(8,128)(2,1)S(1)}, u32[]{:S(2)}, u32[]{:S(2)}) collective-permute-start(bf16[2,64,1024]{2,1,0:T(8,128)(2,1)S(1)} %shard_map.50), channel_id=1, source_target_pairs={{0,1},{1,0},{2,3},{3,2},{4,5},{5,4},{6,7},{7,6},{8,9},{9,8},{10,11... | collective-permute-start | bytes 786440 | tf_op jit(solution)/shard_map/ppermute | solution.py:36
  139.1 15.6 %collective-permute-start.14 = (bf16[2,128,1024]{2,1,0:T(8,128)(2,1)S(1)}, bf16[2,128,1024]{2,1,0:T(8,128)(2,1)S(1)}, u32[]{:S(2)}, u32[]{:S(2)}) collective-permute-start(bf16[2,128,1024]{2,1,0:T(8,128)(2,1)S(1)} %shard_map.51), channel_id=1, source_target_pairs={{0,1},{1,0},{2,3},{3,2},{4,5},{5,4},{6,7},{7,6},{8,9},{9,8},{10,11... | collective-permute-start | bytes 1572872 | tf_op jit(solution)/shard_map/ppermute | solution.py:36
  145.5 7.0 %collective-permute-start.16 = (bf16[2,64,1024]{2,1,0:T(8,128)(2,1)S(1)}, bf16[2,64,1024]{2,1,0:T(8,128)(2,1)S(1)}, u32[]{:S(2)}, u32[]{:S(2)}) collective-permute-start(bf16[2,64,1024]{2,1,0:T(8,128)(2,1)S(1)} %shard_map.52), channel_id=1, source_target_pairs={{0,1},{1,0},{2,3},{3,2},{4,5},{5,4},{6,7},{7,6},{8,9},{9,8},{10,11... | collective-permute-start | bytes 786440 | tf_op jit(solution)/shard_map/ppermute | solution.py:36
  147.6 14.8 %collective-permute-start.17 = (bf16[2,64,1024]{2,1,0:T(8,128)(2,1)S(1)}, bf16[2,64,1024]{2,1,0:T(8,128)(2,1)S(1)}, u32[]{:S(2)}, u32[]{:S(2)}) collective-permute-start(bf16[2,64,1024]{2,1,0:T(8,128)(2,1)S(1)} %add_convert_fusion.2.own.refs_0_), channel_id=1, source_target_pairs={{0,2},{1,3},{2,4},{3,5},{4,6},{5,7},{6,0},{7,1},{8,10},{9,11},{10,... | collective-permute-start | bytes 786440 | tf_op jit(solution)/shard_map/ppermute | solution.py:36
  150.3 14.2 %collective-permute-start.20 = (bf16[2,64,1024]{2,1,0:T(8,128)(2,1)S(1)}, bf16[2,64,1024]{2,1,0:T(8,128)(2,1)S(1)}, u32[]{:S(2)}, u32[]{:S(2)}) collective-permute-start(bf16[2,64,1024]{2,1,0:T(8,128)(2,1)S(1)} %add_convert_fusion.2.own.refs_0_), channel_id=1, source_target_pairs={{0,4},{1,5},{2,6},{3,7},{4,0},{5,1},{6,2},{7,3},{8,12},{9,13},{10,... | collective-permute-start | bytes 786440 | tf_op jit(solution)/shard_map/ppermute | solution.py:36
  151.8 15.4 %collective-permute-start.23 = (bf16[2,64,1024]{2,1,0:T(8,128)(2,1)S(1)}, bf16[2,64,1024]{2,1,0:T(8,128)(2,1)S(1)}, u32[]{:S(2)}, u32[]{:S(2)}) collective-permute-start(bf16[2,64,1024]{2,1,0:T(8,128)(2,1)S(1)} %add_convert_fusion.2.own.refs_0_), channel_id=1, source_target_pairs={{0,6},{1,7},{2,0},{3,1},{4,2},{5,3},{6,4},{7,5},{8,14},{9,15},{10,... | collective-permute-start | bytes 786440 | tf_op jit(solution)/shard_map/ppermute | solution.py:36
  152.6 16.6 %collective-permute-start.19 = (bf16[2,64,1024]{2,1,0:T(8,128)(2,1)S(1)}, bf16[2,64,1024]{2,1,0:T(8,128)(2,1)S(1)}, u32[]{:S(2)}, u32[]{:S(2)}) collective-permute-start(bf16[2,64,1024]{2,1,0:T(8,128)(2,1)S(1)} %add_convert_fusion.1.across.refs_2_), channel_id=1, source_target_pairs={{0,2},{1,3},{2,4},{3,5},{4,6},{5,7},{6,0},{7,1},{8,10},{9,11},{10,... | collective-permute-start | bytes 786440 | tf_op jit(solution)/shard_map/ppermute | solution.py:36
  154.9 31.7 %collective-permute-start.18 = (bf16[2,128,1024]{2,1,0:T(8,128)(2,1)S(1)}, bf16[2,128,1024]{2,1,0:T(8,128)(2,1)S(1)}, u32[]{:S(2)}, u32[]{:S(2)}) collective-permute-start(bf16[2,128,1024]{2,1,0:T(8,128)(2,1)S(1)} %add_convert_fusion.sides.refs_1_), channel_id=1, source_target_pairs={{0,2},{1,3},{2,4},{3,5},{4,6},{5,7},{6,0},{7,1},{8,10},{9,11},{10,... | collective-permute-start | bytes 1572872 | tf_op jit(solution)/shard_map/ppermute | solution.py:36
  162.5 24.2 %collective-permute-start.21 = (bf16[2,128,1024]{2,1,0:T(8,128)(2,1)S(1)}, bf16[2,128,1024]{2,1,0:T(8,128)(2,1)S(1)}, u32[]{:S(2)}, u32[]{:S(2)}) collective-permute-start(bf16[2,128,1024]{2,1,0:T(8,128)(2,1)S(1)} %add_convert_fusion.sides.refs_1_), channel_id=1, source_target_pairs={{0,4},{1,5},{2,6},{3,7},{4,0},{5,1},{6,2},{7,3},{8,12},{9,13},{10,... | collective-permute-start | bytes 1572872 | tf_op jit(solution)/shard_map/ppermute | solution.py:36
  164.5 22.1 %collective-permute-start.24 = (bf16[2,128,1024]{2,1,0:T(8,128)(2,1)S(1)}, bf16[2,128,1024]{2,1,0:T(8,128)(2,1)S(1)}, u32[]{:S(2)}, u32[]{:S(2)}) collective-permute-start(bf16[2,128,1024]{2,1,0:T(8,128)(2,1)S(1)} %add_convert_fusion.sides.refs_1_), channel_id=1, source_target_pairs={{0,6},{1,7},{2,0},{3,1},{4,2},{5,3},{6,4},{7,5},{8,14},{9,15},{10,... | collective-permute-start | bytes 1572872 | tf_op jit(solution)/shard_map/ppermute | solution.py:36
  167.2 16.8 %collective-permute-start.22 = (bf16[2,64,1024]{2,1,0:T(8,128)(2,1)S(1)}, bf16[2,64,1024]{2,1,0:T(8,128)(2,1)S(1)}, u32[]{:S(2)}, u32[]{:S(2)}) collective-permute-start(bf16[2,64,1024]{2,1,0:T(8,128)(2,1)S(1)} %add_convert_fusion.1.across.refs_2_), channel_id=1, source_target_pairs={{0,4},{1,5},{2,6},{3,7},{4,0},{5,1},{6,2},{7,3},{8,12},{9,13},{10,... | collective-permute-start | bytes 786440 | tf_op jit(solution)/shard_map/ppermute | solution.py:36
  169.2 17.4 %collective-permute-start.25 = (bf16[2,64,1024]{2,1,0:T(8,128)(2,1)S(1)}, bf16[2,64,1024]{2,1,0:T(8,128)(2,1)S(1)}, u32[]{:S(2)}, u32[]{:S(2)}) collective-permute-start(bf16[2,64,1024]{2,1,0:T(8,128)(2,1)S(1)} %add_convert_fusion.1.across.refs_2_), channel_id=1, source_target_pairs={{0,6},{1,7},{2,0},{3,1},{4,2},{5,3},{6,4},{7,5},{8,14},{9,15},{10,... | collective-permute-start | bytes 786440 | tf_op jit(solution)/shard_map/ppermute | solution.py:36

commit v2 on v0

v2 whole, which is shorter than its diff:
```python
import jax
import jax.numpy as jnp
from jax import lax
from jax.experimental import pallas as pl
from jax.experimental.pallas import tpu as pltpu
from jax.sharding import PartitionSpec as P

BF16 = jnp.bfloat16
F32 = jnp.float32
PAIR = [(2 * y + p, 2 * y + 1 - p) for y in range(4) for p in range(2)]
CORE = [(0, 1), (1, 0)]
LIMIT = 24 * 1024 * 1024


def along_x(step):
    return [(4 * x + z, 4 * ((x + step) % 4) + z) for x in range(4) for z in range(4)]


def along_z(step):
    return [(4 * x + z, 4 * x + (z + step) % 4) for x in range(4) for z in range(4)]


def along_y(step):
    return [(2 * y + p, 2 * ((y + step) % 4) + p) for y in range(4) for p in range(2)]


def send(value, axis, pairs):
    return lax.ppermute(value, axis, pairs)


def pick(value, index, axis):
    return lax.dynamic_index_in_dim(value, index, axis, keepdims=False)


def choose(distance, candidates):
    out = candidates[0]
    for d in range(1, 4):
        out = jnp.where(distance == d, candidates[d], out)
    return out


def from_below(value, axis, pairs):
    one, three = send(value, axis, pairs(1)), send(value, axis, pairs(3))
    return one, send(value, axis, pairs(2)), three


def tie(value, *others):
    return lax.optimization_barrier((value, *others))[0]


def multiply(chunk, sign, right):
    rows, half = chunk.shape[0], chunk.shape[1] // 2
    turned = jnp.concatenate([-chunk[:, half:], chunk[:, :half]], axis=1) * sign
    left = jnp.concatenate([chunk, turned], axis=0)
    return contract(left, right).astype(BF16).reshape(2, rows, right.shape[0])


def contract(left, right):
    return lax.dot_general(
        left, right, (((1,), (1,)), ((), ())), preferred_element_type=F32
    )


def place_rows(ref, start, value, z):
    for k in range(4):
        to = pl.multiple_of(start + 16 * lax.rem(z + 4 - k, 4), 16)
        ref[pl.ds(to, 16), :] = value[16 * k : 16 * k + 16]


def place_others(ref, value, x, z):
    for d in range(1, 4):
        place_rows(ref, 64 * lax.rem(x + 4 - d, 4), value[64 * d - 64 : 64 * d], z)


def mirror_kernel(place_ref, *refs):
    scratch, out_ref = refs[-1], refs[-2]
    y, x, z = place_ref[0], place_ref[1], place_ref[2]
    sign = jnp.where(pl.program_id(0) == 0, 1.0, -1.0).astype(BF16)
    for d in range(4):
        held = scratch.at[d]
        place_rows(held, 64 * x, refs[2 * d][0], z)
        place_others(held, refs[2 * d + 1][0], x, z)
        columns = pl.ds(pl.multiple_of(256 * lax.rem(y + 4 - d, 4), 256), 256)
        out_ref[0, :, columns] = held[...].T * sign


def mirror(place, held, half, pieces):
    specs = [
        pl.BlockSpec((1, 64, 256), lambda c, t, s: (c, 0, 2 * half + t)),
        pl.BlockSpec((1, 192, 256), lambda c, t, s: (c, 0, t)),
    ] * 4
    operands, aliases = list(pieces), {}
    if held is not None:
        specs.append(pl.BlockSpec(memory_space=pl.ANY))
        operands.append(held)
        aliases = {len(operands): 0}
    return pl.pallas_call(
        mirror_kernel,
        grid_spec=pltpu.PrefetchScalarGridSpec(
            num_scalar_prefetch=1,
            grid=(2, 2),
            in_specs=specs,
            out_specs=pl.BlockSpec((1, 256, 1024), lambda c, t, s: (c, 2 * half + t, 0)),
            scratch_shapes=[pltpu.VMEM((4, 256, 256), BF16)],
        ),
        out_shape=jax.ShapeDtypeStruct((2, 1024, 1024), BF16),
        input_output_aliases=aliases,
        compiler_params=pltpu.CompilerParams(vmem_limit_bytes=LIMIT),
        cost_estimate=pl.CostEstimate(flops=0, bytes_accessed=2**22, transcendentals=0),
    )(place, *operands)


def rows_kernel(place_ref, own, low, high, out_ref, scratch):
    x, z, p = place_ref[1], place_ref[2], place_ref[3]
    place_rows(scratch, 64 * x, own[0], z)
    for half, value in enumerate((low, high)):
        place_others(scratch.at[:, pl.ds(512 * half, 512)], value[0], x, z)
    out_ref[0] = scratch[pl.ds(pl.multiple_of(128 * p, 128), 128), :]


def own_rows(place, pieces):
    return pl.pallas_call(
        rows_kernel,
        grid_spec=pltpu.PrefetchScalarGridSpec(
            num_scalar_prefetch=1,
            grid=(2,),
            in_specs=[
                pl.BlockSpec((1, *piece.shape[1:]), lambda c, s: (c, 0, 0)) for piece in pieces
            ],
            out_specs=pl.BlockSpec((1, 128, 1024), lambda c, s: (c, 0, 0)),
            scratch_shapes=[pltpu.VMEM((256, 1024), BF16)],
        ),
        out_shape=jax.ShapeDtypeStruct((2, 128, 1024), BF16),
        compiler_params=pltpu.CompilerParams(vmem_limit_bytes=LIMIT),
        cost_estimate=pl.CostEstimate(flops=0, bytes_accessed=3 * 2**19, transcendentals=0),
    )(place, *pieces)


def body(pair_density, coulomb, block_index):
    core = lax.axis_index("rows")
    trans = lax.axis_index("trans")
    gvec = lax.axis_index("gvec")
    x, z = trans // 4, trans % 4
    y, p = gvec // 2, gvec % 2
    place = jnp.stack([y, x, z, p]).astype(jnp.int32)
    block = block_index[0]
    other_block = send(block_index, "rows", CORE)[0]

    mine = pick(pair_density, core, 0)
    twin = pick(pair_density, 1 - core, 0)
    below = send(mine, "gvec", along_y(1))
    above = send(mine, "gvec", along_y(3))

    parts = mine.reshape(4, 4, 64, 512)
    got = [pick(parts, x, 1)]
    got += [send(pick(parts, (x + d) % 4, 1), "trans", along_x(d)) for d in (1, 2, 3)]
    swapped = send(choose((x - other_block // 4) % 4, got), "rows", CORE)
    share = jnp.stack([choose((x - block // 4) % 4, got), swapped], axis=1)
    share = (share.astype(F32) * coulomb).astype(BF16)
    share = share.reshape(4, 2, 4, 16, 512)
    got = [pick(share, z, 2)]
    got += [send(pick(share, (z + d) % 4, 2), "trans", along_z(d)) for d in (1, 2, 3)]
    share = choose((z - block % 4) % 4, got)
    low = send(below[:512], "gvec", along_y(1))
    high = send(above[512:], "gvec", along_y(3))
    share = tie(share, low, high)
    below_twin = send(below, "rows", CORE)
    above_twin = send(above, "rows", CORE)
    got = [pick(share, y, 0)]
    got += [send(pick(share, (y + d) % 4, 0), "gvec", along_y(d)) for d in (1, 2, 3)]
    share = jnp.concatenate([piece[c] for c in range(2) for piece in got], axis=1)
    share = tie(share, below_twin, above_twin)
    low_twin = send(low, "rows", CORE)
    high_twin = send(high, "rows", CORE)
    first = [mine, below, None, above, twin, below_twin, None, above_twin]
    right = []
    for half, pair in enumerate(((low, low_twin), (high, high_twin))):
        parts = [v if v is None else v[512 * half : 512 * half + 512] for v in first]
        parts[2], parts[6] = pair
        right.append(jnp.concatenate(parts, axis=1))
    chunk = jnp.concatenate([share, *from_below(share, "trans", along_z)], axis=0)
    chunk, right = lax.optimization_barrier((chunk, right))
    others = from_below(chunk, "trans", along_x)
    sign = (1 - 2 * core).astype(BF16)

    def add(one, other):
        return (one.astype(F32) + other.astype(F32)).astype(BF16)

    own_terms = jnp.concatenate([multiply(chunk, sign, half) for half in right], axis=2)
    own_sum = add(own_terms, send(own_terms, "gvec", PAIR))
    own_piece = (own_sum, *from_below(own_sum, "gvec", along_y))
    others = tie(jnp.concatenate(others), own_sum)
    low_terms = multiply(others, sign, right[0])
    high_terms = multiply(tie(others, low_terms), sign, right[1])
    low_sum = add(low_terms, send(low_terms, "gvec", PAIR))
    low_sum = tie(low_sum, high_terms, *own_piece)
    low_piece = (low_sum, *from_below(low_sum, "gvec", along_y))
    high_sum = add(high_terms, send(high_terms, "gvec", PAIR))
    high_piece = (high_sum, *from_below(high_sum, "gvec", along_y))
    kernel_rows = own_rows(place, (own_sum, low_sum, high_sum))
    mirrored = None
    for half, piece in enumerate((low_piece, high_piece)):
        pieces = [value for d in range(4) for value in (own_piece[d], piece[d])]
        mirrored = mirror(place, mirrored, half, pieces)
    return (kernel_rows, mirrored)


def solution(mesh):
    placed = (P(None, "trans", "gvec"), P("gvec"), P("rows"))
    return jax.shard_map(
        body,
        mesh=mesh,
        in_specs=placed,
        out_specs=(P(None, ("rows", "gvec"), "trans"), P(None, "trans", "rows")),
        check_vma=False,
    )
```

time: 410 us -> 169 us (0.41)
  waiting for transfers between devices: 371 us -> 67.2 us
  starting transfers between devices: 0.12 us -> 55.7 us
  local copies, waits for them, and re-layouts: 6.2 us -> 20.6 us
  between operations: 14.4 us -> 4.51 us
  Pallas kernels: 0 us -> 9.2 us
  other arithmetic: 10.6 us -> 2.76 us
    psum x1 -> x0, waiting for transfers between devices: 181 us -> none  [from_root(): return lax.psum(kept, axis)]
    all_gather x1 -> x0, waiting for transfers between devices: 95.7 us -> none  [body(): gathered = lax.all_gather(kernel_rows, 'gvec', axis=1, tiled=True)]
    reduce_scatter x1 -> x0, waiting for transfers between devices: 94.9 us -> none  [body(): lax.psum_scatter(partial_terms.astype(jnp.bfloat16), 'gvec', scatter_dime...]
    ppermute x0 -> x37, waiting for transfers between devices: none -> 67.2 us  [send(): return lax.ppermute(value, axis, pairs)]
    ppermute x0 -> x37, starting transfers between devices: none -> 55.7 us  [send(): return lax.ppermute(value, axis, pairs)]
    pallas_call x0 -> x3, Pallas kernels: none -> 9.2 us  [the longest x2 7.76 us: mirror(): pl.pallas_call(mirror_kernel, grid_spec=pltpu.PrefetchScalarGridSpec(num_...]
    another operation x3 -> x1, other arithmetic: 7.17 us -> 0.08 us  [body(): place = jnp.stack([y, x, z, p]).astype(jnp.int32)]
    unnamed x5 -> x24, local copies, waits for them, and re-layouts: 6.2 us -> 12.3 us
  transfers between devices with their start and end apart: 3 -> 37, of which waited for: 3 -> 15; matrix products, arithmetic and copies ran while one was open for 0% -> 18% of each run, Pallas kernels for 0% -> 4%
where the time goes in v2:
time: 169 us
  waiting for transfers between devices  67.2 us (40%)
  starting transfers between devices  55.7 us (33%)
  local copies, waits for them, and re-layouts  20.6 us (12%)
  Pallas kernels  9.2 us (5%)
  matrix products  8.94 us (5%)
  between operations  4.51 us (3%)
  other arithmetic  2.76 us (2%)
    ppermute x37, waiting for transfers between devices, send(): return lax.ppermute(value, axis, pairs)  67.2 us
    ppermute x37, starting transfers between devices, send(): return lax.ppermute(value, axis, pairs)  55.7 us
    unnamed x24, local copies, waits for them, and re-layouts  12.3 us
    dot_general x4, matrix products, contract(): lax.dot_general(left, right, (((1,), (1,)), ((), ())), preferred_element_...  8.94 us
    pallas_call x2, Pallas kernels, mirror(): pl.pallas_call(mirror_kernel, grid_spec=pltpu.PrefetchScalarGridSpec(num_...  7.76 us
  transfers between devices with their start and end apart: 37, of which 15 were waited for; matrix products, arithmetic and copies ran while one was open for 18% of the time, Pallas kernels for 4%

profile of v2, /device:TPU:14, one launch (start us, length us, event | category | flops | bytes accessed | tf_op | source)
XLA Modules:
  0.0 168.9 jit_solution(17013841831569993554)
XLA Ops:
  0.6 2.4 %fusion.32 = bf16[1024,512]{1,0:T(8,128)(2,1)} fusion(bf16[2,1024,512]{2,1,0:T(8,128)(2,1)} %param.3, s32[]{:T(128)S(6)} %select_n.190), kind=kLoop, calls=%fused_computation.90 | loop fusion | bytes 2097156 | tf_op jit(solution)/shard_map/jit(dynamic_index_in_dim)/squeeze | solution.py:32
  3.1 1.6 collective-permute-start.8
  5.1 1.3 constant_dynamic-slice_fusion.4
  6.4 0.9 dynamic-slice_bitcast_fusion.4
  7.3 0.8 collective-permute-start
  8.1 1.3 collective-permute-start.1
  9.4 1.9 %collective-permute-start.2 = (bf16[4,64,512]{2,1,0:T(8,128)(2,1)}, bf16[4,64,512]{2,1,0:T(8,128)(2,1)}, u32[]{:S(2)}, u32[]{:S(2)}) collective-permute-start(bf16[4,64,512]{2,1,0:T(8,128)(2,1)} %get-tuple-element.37), channel_id=1, source_target_pairs={{0,32},{8,40},{16,48},{24,56},{32,64},{40,72},{48,80},{56,88},{64,... | collective-permute-start | bytes 786440 | tf_op jit(solution)/shard_map/ppermute | solution.py:28
  12.1 1.1 fusion.15
  16.0 7.1 %collective-permute-done = bf16[4,64,512]{2,1,0:T(8,128)(2,1)S(1)} collective-permute-done((bf16[4,64,512]{2,1,0:T(8,128)(2,1)}, bf16[4,64,512]{2,1,0:T(8,128)(2,1)S(1)}, u32[]{:S(2)}, u32[]{:S(2)}) %collective-permute-start) | collective-permute-done | bytes 262176 | tf_op jit(solution)/shard_map/ppermute | solution.py:28
  23.1 0.7 collective-permute-done.2
  23.8 1.1 fusion.19
  25.0 3.3 %collective-permute-done.8 = bf16[1024,512]{1,0:T(8,128)(2,1)} collective-permute-done((bf16[1024,512]{1,0:T(8,128)(2,1)}, bf16[1024,512]{1,0:T(8,128)(2,1)}, u32[]{:S(2)}, u32[]{:S(2)}) %collective-permute-start.8) | collective-permute-done | bytes 1048608 | tf_op jit(solution)/shard_map/ppermute | solution.py:28
  28.3 2.3 %slice_dynamic-update-slice_fusion.2 = (bf16[512,4096]{1,0:T(8,128)(2,1)}, bf16[512,4096]{1,0:T(8,128)(2,1)}, bf16[512,512]{1,0:T(8,128)(2,1)S(1)}) fusion(bf16[512,4096]{1,0:T(8,128)(2,1)} %get-tuple-element.20, bf16[1024,512]{1,0:T(8,128)(2,1)} %collective-permute-done.8, bf16[512,4096]{1,0:T(8,128)(2,1)} %get-tuple-element.21), kind=kLoop, calls=%fused_computation.25 | loop fusion | bytes 2621440
  30.6 1.6 collective-permute-start.9
  32.2 1.9 %slice.127 = bf16[512,512]{1,0:T(8,128)(2,1)} slice(bf16[1024,512]{1,0:T(8,128)(2,1)} %collective-permute-done.10), slice={[512:1024], [0:512]} | slice | bytes 1048576 | tf_op jit(solution)/shard_map/slice | solution.py:165
  34.7 6.4 %collective-permute-start.5 = (bf16[4,2,16,512]{3,2,1,0:T(8,128)(2,1)S(1)}, bf16[4,2,16,512]{3,2,1,0:T(8,128)(2,1)}, u32[]{:S(2)}, u32[]{:S(2)}) collective-permute-start(bf16[4,2,16,512]{3,2,1,0:T(8,128)(2,1)S(1)} %bitcast.121), channel_id=1, source_target_pairs={{0,24},{8,0},{16,8},{24,16},{32,56},{40,32},{48,40},{56,48},{64,88... | collective-permute-start | bytes 393224 | tf_op jit(solution)/shard_map/ppermute | solution.py:28
  41.1 1.0 collective-permute-start.6
  42.1 0.7 copy.22
  42.8 2.9 %collective-permute-start.7 = (bf16[4,2,16,512]{3,2,1,0:T(8,128)(2,1)}, bf16[4,2,16,512]{3,2,1,0:T(8,128)(2,1)}, u32[]{:S(2)}, u32[]{:S(2)}) collective-permute-start(bf16[4,2,16,512]{3,2,1,0:T(8,128)(2,1)} %bitcast.102), channel_id=1, source_target_pairs={{0,8},{8,16},{16,24},{24,0},{32,40},{40,48},{48,56},{56,32},{64,72... | collective-permute-start | bytes 393224 | tf_op jit(solution)/shard_map/ppermute | solution.py:28
  45.7 5.2 %collective-permute-done.5 = bf16[4,2,16,512]{3,2,1,0:T(8,128)(2,1)} collective-permute-done((bf16[4,2,16,512]{3,2,1,0:T(8,128)(2,1)S(1)}, bf16[4,2,16,512]{3,2,1,0:T(8,128)(2,1)}, u32[]{:S(2)}, u32[]{:S(2)}) %collective-permute-start.5) | collective-permute-done | bytes 131104 | tf_op jit(solution)/shard_map/ppermute | solution.py:28
  50.9 2.1 %collective-permute-done.6 = bf16[4,2,16,512]{3,2,1,0:T(8,128)(2,1)} collective-permute-done((bf16[4,2,16,512]{3,2,1,0:T(8,128)(2,1)S(1)}, bf16[4,2,16,512]{3,2,1,0:T(8,128)(2,1)}, u32[]{:S(2)}, u32[]{:S(2)}) %collective-permute-start.6) | collective-permute-done | bytes 131104 | tf_op jit(solution)/shard_map/ppermute | solution.py:28
  53.7 1.6 collective-permute-start.12
  55.3 3.5 %collective-permute-start.13 = (bf16[2,16,512]{2,1,0:T(8,128)(2,1)S(1)}, bf16[2,16,512]{2,1,0:T(8,128)(2,1)S(1)}, u32[]{:S(2)}, u32[]{:S(2)}) collective-permute-start(bf16[2,16,512]{2,1,0:T(8,128)(2,1)S(1)} %get-tuple-element.47), channel_id=1, source_target_pairs={{0,4},{1,5},{2,6},{3,7},{4,0},{5,1},{6,2},{7,3},{8,12},{9,13},{10,... | collective-permute-start | bytes 98312 | tf_op jit(solution)/shard_map/ppermute | solution.py:28
  58.7 0.9 constant_dynamic-update-slice_fusion.9
  59.6 1.9 %constant_dynamic-update-slice_fusion.13 = bf16[512,4096]{1,0:T(8,128)(2,1)} fusion(bf16[512,4096]{1,0:T(8,128)(2,1)} %get-tuple-element.34, bf16[512,512]{1,0:T(8,128)(2,1)} %collective-permute-done.11), kind=kLoop, calls=%fused_computation.68 | loop fusion | bytes 1048576
  61.5 2.3 %constant_dynamic-update-slice_fusion.12 = (bf16[512,4096]{1,0:T(8,128)(2,1)}, bf16[512,4096]{1,0:T(8,128)(2,1)}) fusion(bf16[512,4096]{1,0:T(8,128)(2,1)} %constant_dynamic-update-slice_fusion.13, bf16[1024,512]{1,0:T(8,128)(2,1)} %collective-permute-done.10, bf16[512,4096]{1,0:T(8,128)(2,1)} %constant_dynamic-update-slice_fusion.9), kind=kLoop, calls=%fused_computation.67 | loop fusion | bytes 2097152
  63.7 1.1 fusion.14
  64.8 0.5 collective-permute-start.21
  65.4 2.8 %collective-permute-start.17 = (bf16[16,4096]{1,0:T(8,128)(2,1)S(1)}, bf16[16,4096]{1,0:T(8,128)(2,1)S(1)}, u32[]{:S(2)}, u32[]{:S(2)}) collective-permute-start(bf16[16,4096]{1,0:T(8,128)(2,1)S(1)} %constant_dynamic-update-slice_fusion), channel_id=1, source_target_pairs={{0,8},{8,16},{16,24},{24,0},{32,40},{40,48},{48,56},{56,32},{64,72... | collective-permute-start | bytes 393224 | tf_op jit(solution)/shard_map/ppermute | solution.py:28
  68.2 4.1 %collective-permute-start.18 = (bf16[16,4096]{1,0:T(8,128)(2,1)S(1)}, bf16[16,4096]{1,0:T(8,128)(2,1)S(1)}, u32[]{:S(2)}, u32[]{:S(2)}) collective-permute-start(bf16[16,4096]{1,0:T(8,128)(2,1)S(1)} %constant_dynamic-update-slice_fusion), channel_id=1, source_target_pairs={{0,16},{8,24},{16,0},{24,8},{32,48},{40,56},{48,32},{56,40},{64,80... | collective-permute-start | bytes 393224 | tf_op jit(solution)/shard_map/ppermute | solution.py:28
  72.3 4.0 %collective-permute-start.19 = (bf16[16,4096]{1,0:T(8,128)(2,1)S(1)}, bf16[16,4096]{1,0:T(8,128)(2,1)S(1)}, u32[]{:S(2)}, u32[]{:S(2)}) collective-permute-start(bf16[16,4096]{1,0:T(8,128)(2,1)S(1)} %constant_dynamic-update-slice_fusion), channel_id=1, source_target_pairs={{0,24},{8,0},{16,8},{24,16},{32,56},{40,32},{48,40},{56,48},{64,88... | collective-permute-start | bytes 393224 | tf_op jit(solution)/shard_map/ppermute | solution.py:28
  76.4 1.1 slice_dynamic-update-slice_fusion.1
  77.5 0.9 constant_dynamic-update-slice_fusion.8
  78.3 0.8 constant_dynamic-update-slice_fusion.11
  79.2 1.1 slice_dynamic-update-slice_fusion
  80.3 1.5 collective-permute-done.18
  81.7 4.8 %collective-permute-done.19 = bf16[16,4096]{1,0:T(8,128)(2,1)S(1)} collective-permute-done((bf16[16,4096]{1,0:T(8,128)(2,1)S(1)}, bf16[16,4096]{1,0:T(8,128)(2,1)S(1)}, u32[]{:S(2)}, u32[]{:S(2)}) %collective-permute-start.19) | collective-permute-done | bytes 131104 | tf_op jit(solution)/shard_map/ppermute | solution.py:28
  86.5 0.8 collective-permute-start.23
  87.4 2.1 %collective-permute-start.24 = (bf16[64,4096]{1,0:T(8,128)(2,1)S(1)}, bf16[64,4096]{1,0:T(8,128)(2,1)S(1)}, u32[]{:S(2)}, u32[]{:S(2)}) collective-permute-start(bf16[64,4096]{1,0:T(8,128)(2,1)S(1)} %pad_maximum_fusion.4), channel_id=1, source_target_pairs={{0,64},{8,72},{16,80},{24,88},{32,96},{40,104},{48,112},{56,120},{... | collective-permute-start | bytes 1572872 | tf_op jit(solution)/shard_map/ppermute | solution.py:28
  89.7 3.7 %convolution_convert_fusion.1 = bf16[128,512]{1,0:T(8,128)(2,1)S(1)} fusion(bf16[512,4096]{1,0:T(8,128)(2,1)} %get-tuple-element.13, bf16[64,4096]{1,0:T(8,128)(2,1)S(1)} %maximum_multiply_fusion.2, bf16[64,4096]{1,0:T(8,128)(2,1)S(1)} %pad_maximum_fusion.4), kind=kOutput, calls=%fused_computation.14 | convolution fusion | flops 539033600 | bytes 5373952 | tf_op jit(solution)/shard_map/dot_general | solution.py:59
  93.4 1.6 convolution_convert_fusion
  95.1 7.7 %collective-permute-done.22 = bf16[2,64,1024]{2,1,0:T(8,128)(2,1)S(1)} collective-permute-done((bf16[2,64,1024]{2,1,0:T(8,128)(2,1)S(1)}, bf16[2,64,1024]{2,1,0:T(8,128)(2,1)S(1)}, u32[]{:S(2)}, u32[]{:S(2)}) %collective-permute-start.22) | collective-permute-done | bytes 262176 | tf_op jit(solution)/shard_map/ppermute | solution.py:28
  102.8 2.1 %collective-permute-start.27 = (bf16[2,64,1024]{2,1,0:T(8,128)(2,1)S(1)}, bf16[2,64,1024]{2,1,0:T(8,128)(2,1)S(1)}, u32[]{:S(2)}, u32[]{:S(2)}) collective-permute-start(bf16[2,64,1024]{2,1,0:T(8,128)(2,1)S(1)} %add_convert_fusion.2.own.refs_0_), channel_id=1, source_target_pairs={{0,2},{1,3},{2,4},{3,5},{4,6},{5,7},{6,0},{7,1},{8,10},{9,11},{10,... | collective-permute-start | bytes 786440 | tf_op jit(solution)/shard_map/ppermute | solution.py:28
  104.9 1.2 collective-permute-start.28
  106.2 0.9 collective-permute-start.29
  107.1 6.6 %collective-permute-done.25 = bf16[64,4096]{1,0:T(8,128)(2,1)S(1)} collective-permute-done((bf16[64,4096]{1,0:T(8,128)(2,1)S(1)}, bf16[64,4096]{1,0:T(8,128)(2,1)S(1)}, u32[]{:S(2)}, u32[]{:S(2)}) %collective-permute-start.25) | collective-permute-done | bytes 524320 | tf_op jit(solution)/shard_map/ppermute | solution.py:28
  114.3 1.8 %fusion.11 = bf16[384,512]{1,0:T(8,128)(2,1)S(1)} fusion(bf16[512,4096]{1,0:T(8,128)(2,1)S(1)} %copy-done.2, bf16[192,4096]{1,0:T(8,128)(2,1)S(1)} %maximum_multiply_fusion, bf16[192,4096]{1,0:T(8,128)(2,1)S(1)} %pad_maximum_fusion), kind=kOutput, calls=%fused_computation.12 | convolution fusion | flops 1617100800 | bytes 7733248 | tf_op jit(solution)/shard_map/dot_general | solution.py:59
  116.7 1.8 %fusion.8 = bf16[384,512]{1,0:T(8,128)(2,1)S(1)} fusion(bf16[512,4096]{1,0:T(8,128)(2,1)S(1)} %copy-done.1, bf16[192,4096]{1,0:T(8,128)(2,1)S(1)} %maximum_multiply_fusion.1, bf16[192,4096]{1,0:T(8,128)(2,1)S(1)} %pad_maximum_fusion), kind=kOutput, calls=%fused_computation.11 | convolution fusion | flops 1617100800 | bytes 7733248 | tf_op jit(solution)/shard_map/dot_general | solution.py:59
  118.5 2.1 %collective-permute-start.30 = (bf16[2,192,512]{2,1,0:T(8,128)(2,1)S(1)}, bf16[2,192,512]{2,1,0:T(8,128)(2,1)S(1)}, u32[]{:S(2)}, u32[]{:S(2)}) collective-permute-start(bf16[2,192,512]{2,1,0:T(8,128)(2,1)S(1)} %bitcast.116), channel_id=1, source_target_pairs={{0,1},{1,0},{2,3},{3,2},{4,5},{5,4},{6,7},{7,6},{8,9},{9,8},{10,11... | collective-permute-start | bytes 1179656 | tf_op jit(solution)/shard_map/ppermute | solution.py:28
  120.6 7.6 %collective-permute-done.26 = bf16[2,192,512]{2,1,0:T(8,128)(2,1)S(1)} collective-permute-done((bf16[2,192,512]{2,1,0:T(8,128)(2,1)S(1)}, bf16[2,192,512]{2,1,0:T(8,128)(2,1)S(1)}, u32[]{:S(2)}, u32[]{:S(2)}) %collective-permute-start.26) | collective-permute-done | bytes 393248 | tf_op jit(solution)/shard_map/ppermute | solution.py:28
  128.3 2.1 %collective-permute-start.34 = (bf16[2,192,512]{2,1,0:T(8,128)(2,1)S(1)}, bf16[2,192,512]{2,1,0:T(8,128)(2,1)S(1)}, u32[]{:S(2)}, u32[]{:S(2)}) collective-permute-start(bf16[2,192,512]{2,1,0:T(8,128)(2,1)S(1)} %add_convert_fusion.1.low.refs_1_), channel_id=1, source_target_pairs={{0,2},{1,3},{2,4},{3,5},{4,6},{5,7},{6,0},{7,1},{8,10},{9,11},{10,... | collective-permute-start | bytes 1179656 | tf_op jit(solution)/shard_map/ppermute | solution.py:28
  130.4 1.4 collective-permute-start.35
  131.8 0.8 collective-permute-start.36
  132.6 3.1 %collective-permute-done.30 = bf16[2,192,512]{2,1,0:T(8,128)(2,1)S(1)} collective-permute-done((bf16[2,192,512]{2,1,0:T(8,128)(2,1)S(1)}, bf16[2,192,512]{2,1,0:T(8,128)(2,1)S(1)}, u32[]{:S(2)}, u32[]{:S(2)}) %collective-permute-start.30) | collective-permute-done | bytes 393248 | tf_op jit(solution)/shard_map/ppermute | solution.py:28
  135.7 2.1 %collective-permute-start.31 = (bf16[2,192,512]{2,1,0:T(8,128)(2,1)S(1)}, bf16[2,192,512]{2,1,0:T(8,128)(2,1)S(1)}, u32[]{:S(2)}, u32[]{:S(2)}) collective-permute-start(bf16[2,192,512]{2,1,0:T(8,128)(2,1)S(1)} %add_convert_fusion.high.refs_1_), channel_id=1, source_target_pairs={{0,2},{1,3},{2,4},{3,5},{4,6},{5,7},{6,0},{7,1},{8,10},{9,11},{10,... | collective-permute-start | bytes 1179656 | tf_op jit(solution)/shard_map/ppermute | solution.py:28
  137.8 1.4 collective-permute-start.32
  139.2 6.8 %collective-permute-done.34.refs_3_ = bf16[2,192,512]{2,1,0:T(8,128)(2,1)S(1)} collective-permute-done((bf16[2,192,512]{2,1,0:T(8,128)(2,1)S(1)}, bf16[2,192,512]{2,1,0:T(8,128)(2,1)S(1)}, u32[]{:S(2)}, u32[]{:S(2)}) %collective-permute-start.34) | collective-permute-done | bytes 393248 | tf_op jit(solution)/shard_map/ppermute | solution.py:28
  146.0 2.8 %collective-permute-start.33 = (bf16[2,192,512]{2,1,0:T(8,128)(2,1)S(1)}, bf16[2,192,512]{2,1,0:T(8,128)(2,1)S(1)}, u32[]{:S(2)}, u32[]{:S(2)}) collective-permute-start(bf16[2,192,512]{2,1,0:T(8,128)(2,1)S(1)} %add_convert_fusion.high.refs_1_), channel_id=1, source_target_pairs={{0,6},{1,7},{2,0},{3,1},{4,2},{5,3},{6,4},{7,5},{8,14},{9,15},{10,... | collective-permute-start | bytes 1179656 | tf_op jit(solution)/shard_map/ppermute | solution.py:28
  148.9 1.4 shard_map.50
  150.4 4.7 %collective-permute-done.36.refs_7_ = bf16[2,192,512]{2,1,0:T(8,128)(2,1)} collective-permute-done((bf16[2,192,512]{2,1,0:T(8,128)(2,1)S(1)}, bf16[2,192,512]{2,1,0:T(8,128)(2,1)}, u32[]{:S(2)}, u32[]{:S(2)}) %collective-permute-start.36) | collective-permute-done | bytes 393248 | tf_op jit(solution)/shard_map/ppermute | solution.py:28
  155.0 4.6 %shard_map.51.refs_8_ = bf16[2,1024,1024]{2,1,0:T(8,128)(2,1)} custom-call(s32[4]{0:T(128)S(1)} %pad_add_fusion.place_ref, bf16[2,64,1024]{2,1,0:T(8,128)(2,1)S(1)} %add_convert_fusion.2.own.refs_0_, bf16[2,192,512]{2,1,0:T(8,128)(2,1)S(1)} %add_convert_fusion.1.low.refs_1_, bf16[2,64,1024]{2,1,0:T(8,128)(2,1)S(1)} %collective-permute-done.27.refs_2_, ...), custom_call_target="tpu_custom_call" | custom-call | bytes 4194304 | tf_op jit(solution)/shard_map/pallas_call | solution.py:97
  159.6 2.9 %collective-permute-done.31.refs_3_ = bf16[2,192,512]{2,1,0:T(8,128)(2,1)S(1)} collective-permute-done((bf16[2,192,512]{2,1,0:T(8,128)(2,1)S(1)}, bf16[2,192,512]{2,1,0:T(8,128)(2,1)S(1)}, u32[]{:S(2)}, u32[]{:S(2)}) %collective-permute-start.31) | collective-permute-done | bytes 393248 | tf_op jit(solution)/shard_map/ppermute | solution.py:28
  162.5 3.3 %collective-permute-done.33.refs_7_ = bf16[2,192,512]{2,1,0:T(8,128)(2,1)S(1)} collective-permute-done((bf16[2,192,512]{2,1,0:T(8,128)(2,1)S(1)}, bf16[2,192,512]{2,1,0:T(8,128)(2,1)S(1)}, u32[]{:S(2)}, u32[]{:S(2)}) %collective-permute-start.33) | collective-permute-done | bytes 393248 | tf_op jit(solution)/shard_map/ppermute | solution.py:28
  165.7 3.2 %shard_map.52 = bf16[2,1024,1024]{2,1,0:T(8,128)(2,1)} custom-call(s32[4]{0:T(128)S(1)} %pad_add_fusion.place_ref, bf16[2,64,1024]{2,1,0:T(8,128)(2,1)S(1)} %add_convert_fusion.2.own.refs_0_, bf16[2,192,512]{2,1,0:T(8,128)(2,1)S(1)} %add_convert_fusion.high.refs_1_, ...), custom_call_target="tpu_custom_call", output_to_operand_aliasing={{}: (9, {})} | custom-call | bytes 4194304 | tf_op jit(solution)/shard_map/pallas_call | solution.py:97
  (68 shorter events, 3.6 us)
Async XLA Ops:
  0.6 11.5 %copy-start = (bf16[2,1024,512]{2,1,0:T(8,128)(2,1)S(1)}, bf16[2,1024,512]{2,1,0:T(8,128)(2,1)}, u32[]{:S(2)}) copy-start(bf16[2,1024,512]{2,1,0:T(8,128)(2,1)} %param.3) | copy-start | bytes 6291460
  3.1 25.2 %collective-permute-start.8 = (bf16[1024,512]{1,0:T(8,128)(2,1)}, bf16[1024,512]{1,0:T(8,128)(2,1)}, u32[]{:S(2)}, u32[]{:S(2)}) collective-permute-start(bf16[1024,512]{1,0:T(8,128)(2,1)} %fusion.32), channel_id=1, source_target_pairs={{0,2},{1,3},{2,4},{3,5},{4,6},{5,7},{6,0},{7,1},{8,10},{9,11},{10,... | collective-permute-start | bytes 3145736 | tf_op jit(solution)/shard_map/ppermute | solution.py:28
  4.6 27.5 %collective-permute-start.10 = (bf16[1024,512]{1,0:T(8,128)(2,1)}, bf16[1024,512]{1,0:T(8,128)(2,1)}, u32[]{:S(2)}, u32[]{:S(2)}) collective-permute-start(bf16[1024,512]{1,0:T(8,128)(2,1)} %fusion.32), channel_id=1, source_target_pairs={{0,6},{1,7},{2,0},{3,1},{4,2},{5,3},{6,4},{7,5},{8,14},{9,15},{10,... | collective-permute-start | bytes 3145736 | tf_op jit(solution)/shard_map/ppermute | solution.py:28
  5.1 4.3 %collective-permute-start.3 = (s32[1]{0:T(128)}, s32[1]{0:T(128)}, u32[]{:S(2)}, u32[]{:S(2)}) collective-permute-start(s32[1]{0:T(128)} %param.5), channel_id=1, source_target_pairs={{0,128},{128,0},{1,129},{129,1},{2,130},{130,2},{3,131},{131,3},{4... | collective-permute-start | bytes 20 | tf_op jit(solution)/shard_map/ppermute | solution.py:28
  7.3 27.2 %copy-start.3 = (f32[512]{0:T(512)S(1)}, f32[512]{0:T(512)}, u32[]{:S(2)}) copy-start(f32[512]{0:T(512)} %param.4) | copy-start | bytes 6148
  7.3 15.8 %collective-permute-start = (bf16[4,64,512]{2,1,0:T(8,128)(2,1)}, bf16[4,64,512]{2,1,0:T(8,128)(2,1)S(1)}, u32[]{:S(2)}, u32[]{:S(2)}) collective-permute-start(bf16[4,64,512]{2,1,0:T(8,128)(2,1)} %get-tuple-element.39), channel_id=1, source_target_pairs={{0,96},{8,104},{16,112},{24,120},{32,0},{40,8},{48,16},{56,24},{64... | collective-permute-start | bytes 786440 | tf_op jit(solution)/shard_map/ppermute | solution.py:28
  8.1 14.9 %collective-permute-start.1 = (bf16[4,64,512]{2,1,0:T(8,128)(2,1)}, bf16[4,64,512]{2,1,0:T(8,128)(2,1)}, u32[]{:S(2)}, u32[]{:S(2)}) collective-permute-start(bf16[4,64,512]{2,1,0:T(8,128)(2,1)} %get-tuple-element.38), channel_id=1, source_target_pairs={{0,64},{8,72},{16,80},{24,88},{32,96},{40,104},{48,112},{56,120},{... | collective-permute-start | bytes 786440 | tf_op jit(solution)/shard_map/ppermute | solution.py:28
  9.4 14.4 %collective-permute-start.2 = (bf16[4,64,512]{2,1,0:T(8,128)(2,1)}, bf16[4,64,512]{2,1,0:T(8,128)(2,1)}, u32[]{:S(2)}, u32[]{:S(2)}) collective-permute-start(bf16[4,64,512]{2,1,0:T(8,128)(2,1)} %get-tuple-element.37), channel_id=1, source_target_pairs={{0,32},{8,40},{16,48},{24,56},{32,64},{40,72},{48,80},{56,88},{64,... | collective-permute-start | bytes 786440 | tf_op jit(solution)/shard_map/ppermute | solution.py:28
  24.9 9.6 %collective-permute-start.4 = (bf16[4,64,512]{2,1,0:T(8,128)(2,1)S(1)}, bf16[4,64,512]{2,1,0:T(8,128)(2,1)S(1)}, u32[]{:S(2)}, u32[]{:S(2)}) collective-permute-start(bf16[4,64,512]{2,1,0:T(8,128)(2,1)S(1)} %get-tuple-element.23), channel_id=1, source_target_pairs={{0,128},{128,0},{1,129},{129,1},{2,130},{130,2},{3,131},{131,3},{4... | collective-permute-start | bytes 786440 | tf_op jit(solution)/shard_map/ppermute | solution.py:28
  30.6 23.1 %collective-permute-start.9 = (bf16[512,512]{1,0:T(8,128)(2,1)S(1)}, bf16[512,512]{1,0:T(8,128)(2,1)S(1)}, u32[]{:S(2)}, u32[]{:S(2)}) collective-permute-start(bf16[512,512]{1,0:T(8,128)(2,1)S(1)} %get-tuple-element.36), channel_id=1, source_target_pairs={{0,2},{1,3},{2,4},{3,5},{4,6},{5,7},{6,0},{7,1},{8,10},{9,11},{10,... | collective-permute-start | bytes 1572872 | tf_op jit(solution)/shard_map/ppermute | solution.py:28
  34.0 19.6 %collective-permute-start.11 = (bf16[512,512]{1,0:T(8,128)(2,1)}, bf16[512,512]{1,0:T(8,128)(2,1)}, u32[]{:S(2)}, u32[]{:S(2)}) collective-permute-start(bf16[512,512]{1,0:T(8,128)(2,1)} %slice.127), channel_id=1, source_target_pairs={{0,6},{1,7},{2,0},{3,1},{4,2},{5,3},{6,4},{7,5},{8,14},{9,15},{10,... | collective-permute-start | bytes 1572872 | tf_op jit(solution)/shard_map/ppermute | solution.py:28
  34.7 16.2 %collective-permute-start.5 = (bf16[4,2,16,512]{3,2,1,0:T(8,128)(2,1)S(1)}, bf16[4,2,16,512]{3,2,1,0:T(8,128)(2,1)}, u32[]{:S(2)}, u32[]{:S(2)}) collective-permute-start(bf16[4,2,16,512]{3,2,1,0:T(8,128)(2,1)S(1)} %bitcast.121), channel_id=1, source_target_pairs={{0,24},{8,0},{16,8},{24,16},{32,56},{40,32},{48,40},{56,48},{64,88... | collective-permute-start | bytes 393224 | tf_op jit(solution)/shard_map/ppermute | solution.py:28
  41.1 11.9 %collective-permute-start.6 = (bf16[4,2,16,512]{3,2,1,0:T(8,128)(2,1)S(1)}, bf16[4,2,16,512]{3,2,1,0:T(8,128)(2,1)}, u32[]{:S(2)}, u32[]{:S(2)}) collective-permute-start(bf16[4,2,16,512]{3,2,1,0:T(8,128)(2,1)S(1)} %bitcast.122), channel_id=1, source_target_pairs={{0,16},{8,24},{16,0},{24,8},{32,48},{40,56},{48,32},{56,40},{64,80... | collective-permute-start | bytes 393224 | tf_op jit(solution)/shard_map/ppermute | solution.py:28
  42.8 10.3 %collective-permute-start.7 = (bf16[4,2,16,512]{3,2,1,0:T(8,128)(2,1)}, bf16[4,2,16,512]{3,2,1,0:T(8,128)(2,1)}, u32[]{:S(2)}, u32[]{:S(2)}) collective-permute-start(bf16[4,2,16,512]{3,2,1,0:T(8,128)(2,1)} %bitcast.102), channel_id=1, source_target_pairs={{0,8},{8,16},{16,24},{24,0},{32,40},{40,48},{48,56},{56,32},{64,72... | collective-permute-start | bytes 393224 | tf_op jit(solution)/shard_map/ppermute | solution.py:28
  53.1 12.3 %collective-permute-start.15 = (bf16[1024,512]{1,0:T(8,128)(2,1)}, bf16[1024,512]{1,0:T(8,128)(2,1)S(1)}, u32[]{:S(2)}, u32[]{:S(2)}) collective-permute-start(bf16[1024,512]{1,0:T(8,128)(2,1)} %collective-permute-done.8), channel_id=1, source_target_pairs={{0,128},{128,0},{1,129},{129,1},{2,130},{130,2},{3,131},{131,3},{4... | collective-permute-start | bytes 3145736 | tf_op jit(solution)/shard_map/ppermute | solution.py:28
  53.2 12.3 %collective-permute-start.16 = (bf16[1024,512]{1,0:T(8,128)(2,1)}, bf16[1024,512]{1,0:T(8,128)(2,1)S(1)}, u32[]{:S(2)}, u32[]{:S(2)}) collective-permute-start(bf16[1024,512]{1,0:T(8,128)(2,1)} %collective-permute-done.10), channel_id=1, source_target_pairs={{0,128},{128,0},{1,129},{129,1},{2,130},{130,2},{3,131},{131,3},{4... | collective-permute-start | bytes 3145736 | tf_op jit(solution)/shard_map/ppermute | solution.py:28
  53.7 11.1 %collective-permute-start.12 = (bf16[2,16,512]{2,1,0:T(8,128)(2,1)S(1)}, bf16[2,16,512]{2,1,0:T(8,128)(2,1)S(1)}, u32[]{:S(2)}, u32[]{:S(2)}) collective-permute-start(bf16[2,16,512]{2,1,0:T(8,128)(2,1)S(1)} %get-tuple-element.48), channel_id=1, source_target_pairs={{0,2},{1,3},{2,4},{3,5},{4,6},{5,7},{6,0},{7,1},{8,10},{9,11},{10,... | collective-permute-start | bytes 98312 | tf_op jit(solution)/shard_map/ppermute | solution.py:28
  55.3 9.5 %collective-permute-start.13 = (bf16[2,16,512]{2,1,0:T(8,128)(2,1)S(1)}, bf16[2,16,512]{2,1,0:T(8,128)(2,1)S(1)}, u32[]{:S(2)}, u32[]{:S(2)}) collective-permute-start(bf16[2,16,512]{2,1,0:T(8,128)(2,1)S(1)} %get-tuple-element.47), channel_id=1, source_target_pairs={{0,4},{1,5},{2,6},{3,7},{4,0},{5,1},{6,2},{7,3},{8,12},{9,13},{10,... | collective-permute-start | bytes 98312 | tf_op jit(solution)/shard_map/ppermute | solution.py:28
  58.7 6.6 %collective-permute-start.14 = (bf16[2,16,512]{2,1,0:T(8,128)(2,1)S(1)}, bf16[2,16,512]{2,1,0:T(8,128)(2,1)S(1)}, u32[]{:S(2)}, u32[]{:S(2)}) collective-permute-start(bf16[2,16,512]{2,1,0:T(8,128)(2,1)S(1)} %get-tuple-element.46), channel_id=1, source_target_pairs={{0,6},{1,7},{2,0},{3,1},{4,2},{5,3},{6,4},{7,5},{8,14},{9,15},{10,... | collective-permute-start | bytes 98312 | tf_op jit(solution)/shard_map/ppermute | solution.py:28
  64.8 12.6 %collective-permute-start.20 = (bf16[512,512]{1,0:T(8,128)(2,1)S(1)}, bf16[512,512]{1,0:T(8,128)(2,1)S(1)}, u32[]{:S(2)}, u32[]{:S(2)}) collective-permute-start(bf16[512,512]{1,0:T(8,128)(2,1)S(1)} %collective-permute-done.9), channel_id=1, source_target_pairs={{0,128},{128,0},{1,129},{129,1},{2,130},{130,2},{3,131},{131,3},{4... | collective-permute-start | bytes 1572872 | tf_op jit(solution)/shard_map/ppermute | solution.py:28
  64.8 13.5 %collective-permute-start.21 = (bf16[512,512]{1,0:T(8,128)(2,1)}, bf16[512,512]{1,0:T(8,128)(2,1)S(1)}, u32[]{:S(2)}, u32[]{:S(2)}) collective-permute-start(bf16[512,512]{1,0:T(8,128)(2,1)} %collective-permute-done.11), channel_id=1, source_target_pairs={{0,128},{128,0},{1,129},{129,1},{2,130},{130,2},{3,131},{131,3},{4... | collective-permute-start | bytes 1572872 | tf_op jit(solution)/shard_map/ppermute | solution.py:28
  65.4 14.8 %collective-permute-start.17 = (bf16[16,4096]{1,0:T(8,128)(2,1)S(1)}, bf16[16,4096]{1,0:T(8,128)(2,1)S(1)}, u32[]{:S(2)}, u32[]{:S(2)}) collective-permute-start(bf16[16,4096]{1,0:T(8,128)(2,1)S(1)} %constant_dynamic-update-slice_fusion), channel_id=1, source_target_pairs={{0,8},{8,16},{16,24},{24,0},{32,40},{40,48},{48,56},{56,32},{64,72... | collective-permute-start | bytes 393224 | tf_op jit(solution)/shard_map/ppermute | solution.py:28
  68.2 13.5 %collective-permute-start.18 = (bf16[16,4096]{1,0:T(8,128)(2,1)S(1)}, bf16[16,4096]{1,0:T(8,128)(2,1)S(1)}, u32[]{:S(2)}, u32[]{:S(2)}) collective-permute-start(bf16[16,4096]{1,0:T(8,128)(2,1)S(1)} %constant_dynamic-update-slice_fusion), channel_id=1, source_target_pairs={{0,16},{8,24},{16,0},{24,8},{32,48},{40,56},{48,32},{56,40},{64,80... | collective-permute-start | bytes 393224 | tf_op jit(solution)/shard_map/ppermute | solution.py:28
  72.3 14.2 %collective-permute-start.19 = (bf16[16,4096]{1,0:T(8,128)(2,1)S(1)}, bf16[16,4096]{1,0:T(8,128)(2,1)S(1)}, u32[]{:S(2)}, u32[]{:S(2)}) collective-permute-start(bf16[16,4096]{1,0:T(8,128)(2,1)S(1)} %constant_dynamic-update-slice_fusion), channel_id=1, source_target_pairs={{0,24},{8,0},{16,8},{24,16},{32,56},{40,32},{48,40},{56,48},{64,88... | collective-permute-start | bytes 393224 | tf_op jit(solution)/shard_map/ppermute | solution.py:28
  80.3 13.2 %copy-start.1 = (bf16[512,4096]{1,0:T(8,128)(2,1)S(1)}, bf16[512,4096]{1,0:T(8,128)(2,1)}, u32[]{:S(2)}) copy-start(bf16[512,4096]{1,0:T(8,128)(2,1)} %get-tuple-element.14) | copy-start | bytes 12582916
  86.5 19.7 %collective-permute-start.23 = (bf16[64,4096]{1,0:T(8,128)(2,1)S(1)}, bf16[64,4096]{1,0:T(8,128)(2,1)S(1)}, u32[]{:S(2)}, u32[]{:S(2)}) collective-permute-start(bf16[64,4096]{1,0:T(8,128)(2,1)S(1)} %pad_maximum_fusion.4), channel_id=1, source_target_pairs={{0,32},{8,40},{16,48},{24,56},{32,64},{40,72},{48,80},{56,88},{64,... | collective-permute-start | bytes 1572872 | tf_op jit(solution)/shard_map/ppermute | solution.py:28
  87.4 19.7 %collective-permute-start.24 = (bf16[64,4096]{1,0:T(8,128)(2,1)S(1)}, bf16[64,4096]{1,0:T(8,128)(2,1)S(1)}, u32[]{:S(2)}, u32[]{:S(2)}) collective-permute-start(bf16[64,4096]{1,0:T(8,128)(2,1)S(1)} %pad_maximum_fusion.4), channel_id=1, source_target_pairs={{0,64},{8,72},{16,80},{24,88},{32,96},{40,104},{48,112},{56,120},{... | collective-permute-start | bytes 1572872 | tf_op jit(solution)/shard_map/ppermute | solution.py:28
  89.5 24.2 %collective-permute-start.25 = (bf16[64,4096]{1,0:T(8,128)(2,1)S(1)}, bf16[64,4096]{1,0:T(8,128)(2,1)S(1)}, u32[]{:S(2)}, u32[]{:S(2)}) collective-permute-start(bf16[64,4096]{1,0:T(8,128)(2,1)S(1)} %pad_maximum_fusion.4), channel_id=1, source_target_pairs={{0,96},{8,104},{16,112},{24,120},{32,0},{40,8},{48,16},{56,24},{64... | collective-permute-start | bytes 1572872 | tf_op jit(solution)/shard_map/ppermute | solution.py:28
  95.0 7.8 %collective-permute-start.22 = (bf16[2,64,1024]{2,1,0:T(8,128)(2,1)S(1)}, bf16[2,64,1024]{2,1,0:T(8,128)(2,1)S(1)}, u32[]{:S(2)}, u32[]{:S(2)}) collective-permute-start(bf16[2,64,1024]{2,1,0:T(8,128)(2,1)S(1)} %pad_maximum_fusion.5), channel_id=1, source_target_pairs={{0,1},{1,0},{2,3},{3,2},{4,5},{5,4},{6,7},{7,6},{8,9},{9,8},{10,11... | collective-permute-start | bytes 786440 | tf_op jit(solution)/shard_map/ppermute | solution.py:28
  102.8 11.4 %copy-start.2 = (bf16[512,4096]{1,0:T(8,128)(2,1)S(1)}, bf16[512,4096]{1,0:T(8,128)(2,1)}, u32[]{:S(2)}) copy-start(bf16[512,4096]{1,0:T(8,128)(2,1)} %get-tuple-element.13) | copy-start | bytes 12582916
  102.8 25.4 %collective-permute-start.27 = (bf16[2,64,1024]{2,1,0:T(8,128)(2,1)S(1)}, bf16[2,64,1024]{2,1,0:T(8,128)(2,1)S(1)}, u32[]{:S(2)}, u32[]{:S(2)}) collective-permute-start(bf16[2,64,1024]{2,1,0:T(8,128)(2,1)S(1)} %add_convert_fusion.2.own.refs_0_), channel_id=1, source_target_pairs={{0,2},{1,3},{2,4},{3,5},{4,6},{5,7},{6,0},{7,1},{8,10},{9,11},{10,... | collective-permute-start | bytes 786440 | tf_op jit(solution)/shard_map/ppermute | solution.py:28
  104.9 23.3 %collective-permute-start.28 = (bf16[2,64,1024]{2,1,0:T(8,128)(2,1)S(1)}, bf16[2,64,1024]{2,1,0:T(8,128)(2,1)S(1)}, u32[]{:S(2)}, u32[]{:S(2)}) collective-permute-start(bf16[2,64,1024]{2,1,0:T(8,128)(2,1)S(1)} %add_convert_fusion.2.own.refs_0_), channel_id=1, source_target_pairs={{0,4},{1,5},{2,6},{3,7},{4,0},{5,1},{6,2},{7,3},{8,12},{9,13},{10,... | collective-permute-start | bytes 786440 | tf_op jit(solution)/shard_map/ppermute | solution.py:28
  106.2 22.1 %collective-permute-start.29 = (bf16[2,64,1024]{2,1,0:T(8,128)(2,1)S(1)}, bf16[2,64,1024]{2,1,0:T(8,128)(2,1)S(1)}, u32[]{:S(2)}, u32[]{:S(2)}) collective-permute-start(bf16[2,64,1024]{2,1,0:T(8,128)(2,1)S(1)} %add_convert_fusion.2.own.refs_0_), channel_id=1, source_target_pairs={{0,6},{1,7},{2,0},{3,1},{4,2},{5,3},{6,4},{7,5},{8,14},{9,15},{10,... | collective-permute-start | bytes 786440 | tf_op jit(solution)/shard_map/ppermute | solution.py:28
  116.1 12.1 %collective-permute-start.26 = (bf16[2,192,512]{2,1,0:T(8,128)(2,1)S(1)}, bf16[2,192,512]{2,1,0:T(8,128)(2,1)S(1)}, u32[]{:S(2)}, u32[]{:S(2)}) collective-permute-start(bf16[2,192,512]{2,1,0:T(8,128)(2,1)S(1)} %bitcast.118), channel_id=1, source_target_pairs={{0,1},{1,0},{2,3},{3,2},{4,5},{5,4},{6,7},{7,6},{8,9},{9,8},{10,11... | collective-permute-start | bytes 1179656 | tf_op jit(solution)/shard_map/ppermute | solution.py:28
  118.5 17.2 %collective-permute-start.30 = (bf16[2,192,512]{2,1,0:T(8,128)(2,1)S(1)}, bf16[2,192,512]{2,1,0:T(8,128)(2,1)S(1)}, u32[]{:S(2)}, u32[]{:S(2)}) collective-permute-start(bf16[2,192,512]{2,1,0:T(8,128)(2,1)S(1)} %bitcast.116), channel_id=1, source_target_pairs={{0,1},{1,0},{2,3},{3,2},{4,5},{5,4},{6,7},{7,6},{8,9},{9,8},{10,11... | collective-permute-start | bytes 1179656 | tf_op jit(solution)/shard_map/ppermute | solution.py:28
  128.3 17.7 %collective-permute-start.34 = (bf16[2,192,512]{2,1,0:T(8,128)(2,1)S(1)}, bf16[2,192,512]{2,1,0:T(8,128)(2,1)S(1)}, u32[]{:S(2)}, u32[]{:S(2)}) collective-permute-start(bf16[2,192,512]{2,1,0:T(8,128)(2,1)S(1)} %add_convert_fusion.1.low.refs_1_), channel_id=1, source_target_pairs={{0,2},{1,3},{2,4},{3,5},{4,6},{5,7},{6,0},{7,1},{8,10},{9,11},{10,... | collective-permute-start | bytes 1179656 | tf_op jit(solution)/shard_map/ppermute | solution.py:28
  130.4 20.0 %collective-permute-start.35 = (bf16[2,192,512]{2,1,0:T(8,128)(2,1)S(1)}, bf16[2,192,512]{2,1,0:T(8,128)(2,1)}, u32[]{:S(2)}, u32[]{:S(2)}) collective-permute-start(bf16[2,192,512]{2,1,0:T(8,128)(2,1)S(1)} %add_convert_fusion.1.low.refs_1_), channel_id=1, source_target_pairs={{0,4},{1,5},{2,6},{3,7},{4,0},{5,1},{6,2},{7,3},{8,12},{9,13},{10,... | collective-permute-start | bytes 1179656 | tf_op jit(solution)/shard_map/ppermute | solution.py:28
  131.8 23.2 %collective-permute-start.36 = (bf16[2,192,512]{2,1,0:T(8,128)(2,1)S(1)}, bf16[2,192,512]{2,1,0:T(8,128)(2,1)}, u32[]{:S(2)}, u32[]{:S(2)}) collective-permute-start(bf16[2,192,512]{2,1,0:T(8,128)(2,1)S(1)} %add_convert_fusion.1.low.refs_1_), channel_id=1, source_target_pairs={{0,6},{1,7},{2,0},{3,1},{4,2},{5,3},{6,4},{7,5},{8,14},{9,15},{10,... | collective-permute-start | bytes 1179656 | tf_op jit(solution)/shard_map/ppermute | solution.py:28
  135.7 26.7 %collective-permute-start.31 = (bf16[2,192,512]{2,1,0:T(8,128)(2,1)S(1)}, bf16[2,192,512]{2,1,0:T(8,128)(2,1)S(1)}, u32[]{:S(2)}, u32[]{:S(2)}) collective-permute-start(bf16[2,192,512]{2,1,0:T(8,128)(2,1)S(1)} %add_convert_fusion.high.refs_1_), channel_id=1, source_target_pairs={{0,2},{1,3},{2,4},{3,5},{4,6},{5,7},{6,0},{7,1},{8,10},{9,11},{10,... | collective-permute-start | bytes 1179656 | tf_op jit(solution)/shard_map/ppermute | solution.py:28
  137.8 24.6 %collective-permute-start.32 = (bf16[2,192,512]{2,1,0:T(8,128)(2,1)S(1)}, bf16[2,192,512]{2,1,0:T(8,128)(2,1)S(1)}, u32[]{:S(2)}, u32[]{:S(2)}) collective-permute-start(bf16[2,192,512]{2,1,0:T(8,128)(2,1)S(1)} %add_convert_fusion.high.refs_1_), channel_id=1, source_target_pairs={{0,4},{1,5},{2,6},{3,7},{4,0},{5,1},{6,2},{7,3},{8,12},{9,13},{10,... | collective-permute-start | bytes 1179656 | tf_op jit(solution)/shard_map/ppermute | solution.py:28
  146.0 19.7 %collective-permute-start.33 = (bf16[2,192,512]{2,1,0:T(8,128)(2,1)S(1)}, bf16[2,192,512]{2,1,0:T(8,128)(2,1)S(1)}, u32[]{:S(2)}, u32[]{:S(2)}) collective-permute-start(bf16[2,192,512]{2,1,0:T(8,128)(2,1)S(1)} %add_convert_fusion.high.refs_1_), channel_id=1, source_target_pairs={{0,6},{1,7},{2,0},{3,1},{4,2},{5,3},{6,4},{7,5},{8,14},{9,15},{10,... | collective-permute-start | bytes 1179656 | tf_op jit(solution)/shard_map/ppermute | solution.py:28
